TPU v7x, 32 devices: a whole 2x2x4 slice. The times are simulated.
32 devices in a mesh: groups: 2 (over y), op: 4 (over z), sec: 2 (over x), help: 2 (over core).
Axes of the slice: x: 2, y: 2, z: 4, core: 2. Of those that a mesh axis runs over, the one named last changes fastest.
Arguments:
- psi_one: bfloat16 [16, 256, 256], P(('groups', 'sec'), ('op', 'help')), parts along dimension 0, may hold values from -6 to 6
- psi_two: bfloat16 [16, 256, 256], P(('groups', 'sec'), ('op', 'help')), parts along dimension 0, may hold values from -6 to 6
- left_blocks: bfloat16 [64, 256, 256], P(('groups', 'op')), parts along dimension 0, may hold values from -0.375 to 0.375
- right_blocks: bfloat16 [64, 256, 256], P(('groups', 'op')), parts along dimension 0, may hold values from -0.046875 to 0.046875
- task_in: int32 [8, 2, 64], P(('groups', 'op'), 'sec'), parts along dimension 0, may hold values from 0 to 3
- task_out: int32 [8, 2, 64], P(('groups', 'op'), 'sec'), parts along dimension 0, may hold values from 0 to 3
- task_left: int32 [8, 2, 64], P(('groups', 'op'), 'sec'), parts along dimension 0, may hold values from 0 to 7
- task_right: int32 [8, 2, 64], P(('groups', 'op'), 'sec'), parts along dimension 0, may hold values from 0 to 7
- task_count: int32 [8, 2], P(('groups', 'op'), 'sec'), parts along dimension 0, may hold values from 16 to 64
Outputs:
- sigma_one: float32 [16, 256, 256], P(('groups', 'sec'), ('op', 'help')), parts along dimension 0
- sigma_two: float32 [16, 256, 256], P(('groups', 'sec'), ('op', 'help')), parts along dimension 0
- subspace: float32 [4, 2], P('groups'), parts along dimension 0
There are 2 independent parts, one for each index of `groups`. A program takes and returns all parts, laid end to end along the dimension named above; each array names one. Nothing has to cross between parts.
All inputs are finite; a program needn't handle non-finite values.
Results may differ from a plain program's by a relative error of at most 0.0029.
Values may be sent and summed in bfloat16 or wider, within the bound.
No kernel may reach another device: no remote copies, remote signals or barrier semaphores. Data moves between devices by JAX's collectives and lax.ppermute only.
A program may use at most 64 MiB of HBM per device.

v0:
```python
import functools
import math

import jax
import jax.numpy as jnp
from jax import lax
from jax.experimental import pallas as pl
from jax.experimental.pallas import tpu as pltpu
from jax.sharding import PartitionSpec as P

F32 = jnp.float32
BF16 = jnp.bfloat16
SCALARS = pl.BlockSpec(memory_space=pltpu.SMEM)
VECTORS = pl.BlockSpec(memory_space=pltpu.VMEM)
MIB = 1024 * 1024


def call(kernel, outs, args, n_scalars, mib, name, scratch=(), flops=0):
    return pl.pallas_call(
        kernel,
        out_shape=outs,
        in_specs=[SCALARS] * n_scalars + [VECTORS] * (len(args) - n_scalars),
        out_specs=jax.tree.map(lambda _: VECTORS, outs),
        scratch_shapes=list(scratch),
        compiler_params=pltpu.CompilerParams(vmem_limit_bytes=mib * MIB),
        cost_estimate=pl.CostEstimate(flops=flops, bytes_accessed=0, transcendentals=0) if flops else None,
        name=name,
    )(*args)


def tile_of(x):
    total = None
    for r in range(0, x.shape[0], 8):
        for c in range(0, x.shape[1], 128):
            part = x[r : r + 8, c : c + 128]
            total = part if total is None else total + part
    return total


def dots_of(me, near, sums):
    sectors, n_op = sums.shape[0], sums.shape[2]
    dots = [[None, None], [None, None]]
    for k in range(n_op):
        for c in range(sectors):
            parts = [sums[c, w, me ^ k] for w in range(2)]
            for v in range(2):
                wave = near[v][k][c].astype(F32)
                for w in range(2):
                    part = tile_of(wave * parts[w])
                    dots[v][w] = part if dots[v][w] is None else dots[v][w] + part
    row = lax.broadcasted_iota(jnp.int32, (8, 128), 0)
    lane = lax.broadcasted_iota(jnp.int32, (8, 128), 1)
    tile = jnp.zeros((8, 128), F32)
    for v in range(2):
        for w in range(2):
            tile = jnp.where((row == v) & (lane == w), jnp.sum(dots[v][w]), tile)
    return tile


def to_wire(tile, width):
    high = tile.astype(BF16).astype(F32)
    middle = (tile - high).astype(BF16).astype(F32)
    low = tile - high - middle
    parts = jnp.concatenate([high[:2], middle[:2], low[:2], jnp.zeros((10, 128), F32)])
    return jnp.concatenate([parts] * (width // 128), axis=1).astype(BF16)


def from_wire(ref, at):
    parts = ref[at:, :128].astype(F32)
    two = parts[0:2] + parts[2:4] + parts[4:6]
    return jnp.concatenate([two, jnp.zeros((6, 128), F32)])


def add_tasks(batch, table, left_ref, right_ref, waves, inner, sums):
    sectors, _, n_op, rows, width = sums.shape
    ops, half = right_ref.shape[0], n_op * rows
    left = left_ref[...].reshape(ops * half, width)
    for a in range(sectors):
        for v in range(2):
            found = jnp.dot(left, waves[v, a], preferred_element_type=F32).astype(BF16)
            inner[pl.ds(a * ops, ops), v] = found.reshape(ops, half, width)
    inner[sectors * ops] = jnp.zeros((2, half, width), BF16)
    sums[...] = jnp.zeros_like(sums)

    def step(g, carry):
        for i in range(batch):
            t = g * batch + i
            block = inner[table[0, t]].reshape(2 * half, width)
            found = jnp.dot(block, right_ref[table[1, t]], preferred_element_type=F32)
            sums[table[2, t]] += found.reshape(2, n_op, rows, width)
        return carry

    lax.fori_loop(0, (table[3, 2] + batch - 1) // batch, step, 0)


def fast_kernel(batch, table, left_ref, right_ref, *refs):
    waves_in, refs = refs[:16], refs[16:]
    *outs, dots_ref, waves, inner, sums = refs
    rows = sums.shape[3]
    me, helper = table[3, 0], table[3, 1]
    for v in range(2):
        for k in range(4):
            for other in range(2):
                owner = helper if other == 0 else 1 - helper
                at = pl.multiple_of(((me ^ k) * 2 + owner) * rows, rows)
                waves[v, :, pl.ds(at, rows), :] = waves_in[v * 8 + other * 4 + k][...]
    add_tasks(batch, table, left_ref, right_ref, waves, inner, sums)
    n = sums.shape[0] * rows
    for v in range(2):
        for k in range(4):
            part = sums[:, v, me ^ k].reshape(n, -1)
            outs[4 * v + k][:n] = part if k == 0 else part.astype(BF16)
    tile = dots_of(me, (waves_in[:4], waves_in[8:12]), sums)
    dots_ref[...] = tile
    wire = to_wire(tile, sums.shape[-1])
    for k in range(1, 4):
        outs[k][n:] = wire


def fast_products(batch, table, left, right, waves):
    ops, n_op, rows, width = left.shape
    sectors = waves[0].shape[0]
    outs = []
    for v in range(2):
        n = sectors * rows
        outs.append(jax.ShapeDtypeStruct((n, width), F32))
        outs += [jax.ShapeDtypeStruct((n + (16 if v == 0 else 0), width), BF16)] * 3
    outs.append(jax.ShapeDtypeStruct((8, 128), F32))
    scratch = [
        pltpu.VMEM((2, sectors, width, width), BF16),
        pltpu.VMEM((sectors * ops + 1, 2, n_op * rows, width), BF16),
        pltpu.VMEM((sectors, 2, n_op, rows, width), F32),
    ]
    kernel = functools.partial(fast_kernel, batch)
    return call(kernel, outs, [table, left, right, *waves], 1, 20, "products", scratch)


def any_kernel(batch, table, left_ref, right_ref, waves, sums, inner):
    add_tasks(batch, table, left_ref, right_ref, waves, inner, sums)


def any_products(batch, table, left, right, waves):
    ops, n_op, rows, width = left.shape
    sectors = waves.shape[1]
    out = jax.ShapeDtypeStruct((sectors, 2, n_op, rows, width), F32)
    scratch = [pltpu.VMEM((sectors * ops + 1, 2, n_op * rows, width), BF16)]
    kernel = functools.partial(any_kernel, batch)
    return call(kernel, out, [table, left, right, waves], 1, 20, "products", scratch)


def add_up(terms):
    while len(terms) > 1:
        terms = [a + b for a, b in zip(terms[::2], terms[1::2])]
    return terms[0]


def dots_kernel(n, own, *refs):
    refs[-1][...] = add_up([own[...]] + [from_wire(r, n) for r in refs[:-1]])


def all_dots(own, received):
    kernel = functools.partial(dots_kernel, received[0].shape[0] - 16)
    return call(kernel, jax.ShapeDtypeStruct((8, 128), F32), [own, *received], 0, 1, "all_dots")


def finish_kernel(mine, *refs):
    received, out = refs[:-1], refs[-1]
    n = mine.shape[0]
    total = mine[...]
    for part in received:
        total = total + part[:n].astype(F32)
    out[...] = total.reshape(out.shape)


def finish(shape, mine, received):
    out = jax.ShapeDtypeStruct(shape, F32)
    return call(finish_kernel, out, [mine, *received], 0, 4, "finish")


def subspace_kernel(scale, *refs):
    refs[-1][...] = add_up([t[:2, :2] for t in refs[:-1]]) * scale


def subspace_of(scale, terms):
    out = jax.ShapeDtypeStruct((2, 2), F32)
    return call(functools.partial(subspace_kernel, scale), out, terms, 0, 1, "subspace")


def terms_of(x, axes):
    size = math.prod(lax.axis_size(a) for a in axes)
    terms, hop = [x], 1
    while hop < size:
        x = add_up(terms)
        hops = [hop] if hop * 2 == size else [hop, 2 * hop, 3 * hop]
        terms = [x] + [swap(x, axes, h) for h in hops]
        hop *= 1 + len(hops)
    return terms


def swap(x, axes, hop):
    size = math.prod(lax.axis_size(a) for a in axes)
    return lax.ppermute(x, axes, [(i, i ^ hop) for i in range(size)])


def after(x, y):
    return lax.optimization_barrier((x, y))


def fast(psi_one, psi_two, left, right, table, batch, scale):
    op, core = ("op",), ("help",)
    psi = (psi_one, psi_two)
    waves = []
    far = [swap(x, op, 2) for x in psi]
    later, left = after(psi, left)
    near = [[psi[v], swap(later[v], op, 1), far[v], swap(far[v], op, 1)] for v in range(2)]
    for v in range(2):
        waves += near[v] + [swap(x, core, 1) for x in near[v]]
    *parts, dots = fast_products(batch, table, left, right, waves)
    first = [swap(x, op, k + 1) for k, x in enumerate(parts[1:4])]
    second = [swap(x, op, k + 1) for k, x in enumerate(parts[5:8])]
    terms = terms_of(all_dots(dots, first), ("sec", "help"))
    sigma_one = finish(psi_one.shape, parts[0], first)
    second, sigma_one = after(second, sigma_one)
    sigma_two = finish(psi_two.shape, parts[4], second)
    return sigma_one, sigma_two, subspace_of(scale, terms)


def general(psi_one, psi_two, left, right, table, batch, scale):
    n_op = lax.axis_size("op")
    me = lax.axis_index("op")
    own = jnp.stack([psi_one, psi_two])
    waves = lax.all_gather(own, ("op", "help"), axis=2, tiled=True)
    sums = jnp.swapaxes(any_products(batch, table, left, right, waves), 0, 1)
    total = jnp.take(sums, me, axis=2)
    for k in range(1, n_op):
        sent = jnp.take(sums, (me + k) % n_op, axis=2).astype(BF16)
        moved = lax.ppermute(sent, "op", [(i, (i + k) % n_op) for i in range(n_op)])
        total = total + moved.astype(F32)
    rows = psi_one.shape[1]
    parts = waves.reshape(*waves.shape[:2], n_op, 2, rows, waves.shape[-1])
    mine = jnp.take(parts, lax.axis_index("help"), axis=3).astype(F32)
    dots = jnp.einsum("vsoab,wsoab->vw", mine, sums, precision=lax.Precision.HIGHEST)
    return total[0], total[1], lax.psum(dots, ("op", "sec", "help")) * scale


def local(
    psi_one,
    psi_two,
    left_blocks,
    right_blocks,
    task_in,
    task_out,
    task_left,
    task_right,
    task_count,
):
    sectors, rows, width = psi_one.shape
    ops = left_blocks.shape[0]
    slots = task_in.shape[-1]
    n_op = lax.axis_size("op")
    me = lax.axis_index("op")
    helper = lax.axis_index("help")
    slot = jnp.arange(slots, dtype=jnp.int32)
    flat = lambda t: t.reshape(slots)
    live = task_count.reshape(())
    block = jnp.where(slot < live, flat(task_in) * ops + flat(task_left), sectors * ops)
    state = jnp.where(slot == 0, me, jnp.where(slot == 1, helper, live)).astype(jnp.int32)
    table = jnp.stack([block, flat(task_right), flat(task_out), state])
    lefts = left_blocks.reshape(ops, n_op, 2, rows, width)
    left = jnp.take(lefts, helper, axis=2)
    right = jnp.swapaxes(right_blocks, 1, 2)
    batch = math.gcd(slots, 16)
    scale = 1.0 / math.sqrt(sectors * lax.axis_size("sec") * width * width)
    way = fast if n_op == 4 and rows % 16 == 0 else general
    return way(psi_one, psi_two, left, right, table, batch, scale)


def solution(mesh):
    placed = (
        P(("groups", "sec"), ("op", "help"), None),
        P(("groups", "sec"), ("op", "help"), None),
        P(("groups", "op"), None, None),
        P(("groups", "op"), None, None),
        P(("groups", "op"), "sec", None),
        P(("groups", "op"), "sec", None),
        P(("groups", "op"), "sec", None),
        P(("groups", "op"), "sec", None),
        P(("groups", "op"), "sec"),
    )
    return jax.shard_map(
        local,
        mesh=mesh,
        in_specs=placed,
        out_specs=(
            P(("groups", "sec"), ("op", "help"), None),
            P(("groups", "sec"), ("op", "help"), None),
            P("groups", None),
        ),
        check_vma=False,
    )
```

profile of v0, /device:TPU:0, one launch (start us, length us, event | category | flops | bytes accessed | tf_op | source)
XLA Modules:
  0.0 40.9 jit_solution(15803133784760740187)
XLA Ops:
  0.6 4.1 %collective-permute-start.1 = (bf16[4,32,256]{2,1,0:T(8,128)(2,1)}, bf16[4,32,256]{2,1,0:T(8,128)(2,1)S(1)}, u32[]{:S(2)}, u32[]{:S(2)}) collective-permute-start(bf16[4,32,256]{2,1,0:T(8,128)(2,1)} %refs_0_.1), channel_id=1, source_target_pairs={{0,8},{4,12},{8,0},{12,4},{1,9},{5,13},{9,1},{13,5},{2,10},{6,14},... | collective-permute-start | bytes 196616 | tf_op jit(solution)/shard_map/ppermute | solution.py:202
  4.7 0.2 collective-permute-start.8
  4.9 0.4 collective-permute-start.10
  5.3 1.1 %fusion.left_ref = bf16[8,4,32,256]{3,2,1,0:T(8,128)(2,1)S(1)} fusion(bf16[8,4,2,32,256]{4,3,2,1,0:T(8,128)(2,1)} %bitcast.15, s32[]{:T(128)S(6)} %select_n.45, pred[]{:T(512)S(6)} %and.7), kind=kLoop, calls=%fused_computation.1 | loop fusion | flops 262144 | bytes 1048581 | tf_op jit(solution)/shard_map/jit(_take)/select_n | solution.py:270
  6.4 1.7 %collective-permute-start = (bf16[4,32,256]{2,1,0:T(8,128)(2,1)S(1)}, bf16[4,32,256]{2,1,0:T(8,128)(2,1)S(1)}, u32[]{:S(2)}, u32[]{:S(2)}) collective-permute-start(bf16[4,32,256]{2,1,0:T(8,128)(2,1)S(1)} %copy-done), channel_id=1, source_target_pairs={{0,4},{4,0},{8,12},{12,8},{1,5},{5,1},{9,13},{13,9},{2,6},{6,2},{1... | collective-permute-start | bytes 196616 | tf_op jit(solution)/shard_map/ppermute | solution.py:202
  8.8 2.1 %collective-permute-start.7 = (bf16[4,32,256]{2,1,0:T(8,128)(2,1)S(1)}, bf16[4,32,256]{2,1,0:T(8,128)(2,1)S(1)}, u32[]{:S(2)}, u32[]{:S(2)}) collective-permute-start(bf16[4,32,256]{2,1,0:T(8,128)(2,1)S(1)} %copy-done.1), channel_id=1, source_target_pairs={{0,4},{4,0},{8,12},{12,8},{1,5},{5,1},{9,13},{13,9},{2,6},{6,2},{1... | collective-permute-start | bytes 196616 | tf_op jit(solution)/shard_map/ppermute | solution.py:202
  10.9 0.8 %collective-permute-done.8.refs_10_ = bf16[4,32,256]{2,1,0:T(8,128)(2,1)S(1)} collective-permute-done((bf16[4,32,256]{2,1,0:T(8,128)(2,1)}, bf16[4,32,256]{2,1,0:T(8,128)(2,1)S(1)}, u32[]{:S(2)}, u32[]{:S(2)}) %collective-permute-start.8) | collective-permute-done | bytes 65568 | tf_op jit(solution)/shard_map/ppermute | solution.py:202
  11.8 0.3 collective-permute-start.2
  12.1 1.7 %collective-permute-start.9 = (bf16[4,32,256]{2,1,0:T(8,128)(2,1)S(1)}, bf16[4,32,256]{2,1,0:T(8,128)(2,1)S(1)}, u32[]{:S(2)}, u32[]{:S(2)}) collective-permute-start(bf16[4,32,256]{2,1,0:T(8,128)(2,1)S(1)} %collective-permute-done.8.refs_10_), channel_id=1, source_target_pairs={{0,4},{4,0},{8,12},{12,8},{1,5},{5,1},{9,13},{13,9},{2,6},{6,2},{1... | collective-permute-start | bytes 196616 | tf_op jit(solution)/shard_map/ppermute | solution.py:202
  13.8 1.5 %copy.14 = bf16[8,256,256]{1,2,0:T(8,128)(2,1)S(1)} copy(bf16[8,256,256]{2,1,0:T(8,128)(2,1)} %param.12) | data formatting | bytes 2097152 | tf_op args[3]
  15.3 0.1 collective-permute-start.12
  15.4 0.5 %collective-permute-start.4 = (bf16[4,32,256]{2,1,0:T(8,128)(2,1)S(1)}, bf16[4,32,256]{2,1,0:T(8,128)(2,1)S(1)}, u32[]{:S(2)}, u32[]{:S(2)}) collective-permute-start(bf16[4,32,256]{2,1,0:T(8,128)(2,1)S(1)} %collective-permute-done.refs_1_), channel_id=1, source_target_pairs={{0,1},{1,0},{2,3},{3,2},{4,5},{5,4},{6,7},{7,6},{8,9},{9,8},{10,11... | collective-permute-start | bytes 196616 | tf_op jit(solution)/shard_map/ppermute | solution.py:202
  15.9 0.1 collective-permute-start.11
  16.0 0.2 collective-permute-done.2.refs_3_
  16.1 0.3 collective-permute-start.6
  16.4 0.4 %collective-permute-done.9.refs_11_ = bf16[4,32,256]{2,1,0:T(8,128)(2,1)S(1)} collective-permute-done((bf16[4,32,256]{2,1,0:T(8,128)(2,1)S(1)}, bf16[4,32,256]{2,1,0:T(8,128)(2,1)S(1)}, u32[]{:S(2)}, u32[]{:S(2)}) %collective-permute-start.9) | collective-permute-done | bytes 65568 | tf_op jit(solution)/shard_map/ppermute | solution.py:202
  16.9 0.7 %copy-done.4 = s32[1,1,64]{2,1,0:T(1,128)S(1)} copy-done((s32[1,1,64]{2,1,0:T(1,128)S(1)}, s32[1,1,64]{2,1,0:T(1,128)}, u32[]{:S(2)}) %copy-start.4) | copy-done | bytes 280
  17.6 0.5 %collective-permute-done.13.refs_15_ = bf16[4,32,256]{2,1,0:T(8,128)(2,1)S(1)} collective-permute-done((bf16[4,32,256]{2,1,0:T(8,128)(2,1)S(1)}, bf16[4,32,256]{2,1,0:T(8,128)(2,1)S(1)}, u32[]{:S(2)}, u32[]{:S(2)}) %collective-permute-start.13) | collective-permute-done | bytes 65568 | tf_op jit(solution)/shard_map/ppermute | solution.py:202
  18.1 3.0 %products.1 = (f32[128,256]{1,0:T(8,128)S(1)}, bf16[144,256]{1,0:T(8,128)(2,1)S(1)}, bf16[144,256]{1,0:T(8,128)(2,1)S(1)}, bf16[144,256]{1,0:T(8,128)(2,1)S(1)},...) custom-call(s32[4,64]{1,0:T(4,128)S(1)} %pad_add_fusion.table, ...), custom_call_target="tpu_custom_call" | custom-call | tf_op jit(solution)/shard_map/products/pallas_call | solution.py:19
  21.1 3.6 %collective-permute-start.17 = (bf16[144,256]{1,0:T(8,128)(2,1)S(1)}, bf16[144,256]{1,0:T(8,128)(2,1)S(1)}, u32[]{:S(2)}, u32[]{:S(2)}) collective-permute-start(bf16[144,256]{1,0:T(8,128)(2,1)S(1)} %get-tuple-element.26), channel_id=1, source_target_pairs={{0,4},{4,0},{8,12},{12,8},{1,5},{5,1},{9,13},{13,9},{2,6},{6,2},{1... | collective-permute-start | bytes 221192 | tf_op jit(solution)/shard_map/ppermute | solution.py:202
  24.7 2.5 %collective-permute-start.18 = (bf16[144,256]{1,0:T(8,128)(2,1)S(1)}, bf16[144,256]{1,0:T(8,128)(2,1)S(1)}, u32[]{:S(2)}, u32[]{:S(2)}) collective-permute-start(bf16[144,256]{1,0:T(8,128)(2,1)S(1)} %get-tuple-element.27), channel_id=1, source_target_pairs={{0,8},{4,12},{8,0},{12,4},{1,9},{5,13},{9,1},{13,5},{2,10},{6,14},... | collective-permute-start | bytes 221192 | tf_op jit(solution)/shard_map/ppermute | solution.py:202
  27.2 1.1 %collective-permute-start.19 = (bf16[144,256]{1,0:T(8,128)(2,1)S(1)}, bf16[144,256]{1,0:T(8,128)(2,1)S(1)}, u32[]{:S(2)}, u32[]{:S(2)}) collective-permute-start(bf16[144,256]{1,0:T(8,128)(2,1)S(1)} %get-tuple-element.28), channel_id=1, source_target_pairs={{0,12},{4,8},{8,4},{12,0},{1,13},{5,9},{9,5},{13,1},{2,14},{6,10},... | collective-permute-start | bytes 221192 | tf_op jit(solution)/shard_map/ppermute | solution.py:202
  28.3 0.6 %collective-permute-start.14 = (bf16[128,256]{1,0:T(8,128)(2,1)S(1)}, bf16[128,256]{1,0:T(8,128)(2,1)S(1)}, u32[]{:S(2)}, u32[]{:S(2)}) collective-permute-start(bf16[128,256]{1,0:T(8,128)(2,1)S(1)} %get-tuple-element.22), channel_id=1, source_target_pairs={{0,4},{4,0},{8,12},{12,8},{1,5},{5,1},{9,13},{13,9},{2,6},{6,2},{1... | collective-permute-start | bytes 196616 | tf_op jit(solution)/shard_map/ppermute | solution.py:202
  28.9 2.7 %collective-permute-start.15 = (bf16[128,256]{1,0:T(8,128)(2,1)S(1)}, bf16[128,256]{1,0:T(8,128)(2,1)S(1)}, u32[]{:S(2)}, u32[]{:S(2)}) collective-permute-start(bf16[128,256]{1,0:T(8,128)(2,1)S(1)} %get-tuple-element.23), channel_id=1, source_target_pairs={{0,8},{4,12},{8,0},{12,4},{1,9},{5,13},{9,1},{13,5},{2,10},{6,14},... | collective-permute-start | bytes 196616 | tf_op jit(solution)/shard_map/ppermute | solution.py:202
  31.6 1.1 %collective-permute-start.16 = (bf16[128,256]{1,0:T(8,128)(2,1)S(1)}, bf16[128,256]{1,0:T(8,128)(2,1)S(1)}, u32[]{:S(2)}, u32[]{:S(2)}) collective-permute-start(bf16[128,256]{1,0:T(8,128)(2,1)S(1)} %get-tuple-element.24), channel_id=1, source_target_pairs={{0,12},{4,8},{8,4},{12,0},{1,13},{5,9},{9,5},{13,1},{2,14},{6,10},... | collective-permute-start | bytes 196616 | tf_op jit(solution)/shard_map/ppermute | solution.py:202
  32.7 1.8 %collective-permute-done.19.refs_2_ = bf16[144,256]{1,0:T(8,128)(2,1)S(1)} collective-permute-done((bf16[144,256]{1,0:T(8,128)(2,1)S(1)}, bf16[144,256]{1,0:T(8,128)(2,1)S(1)}, u32[]{:S(2)}, u32[]{:S(2)}) %collective-permute-start.19) | collective-permute-done | bytes 73760 | tf_op jit(solution)/shard_map/ppermute | solution.py:202
  34.6 0.1 collective-permute-start.22
  34.6 1.9 %collective-permute-start.21 = (f32[8,128]{1,0:T(8,128)S(1)}, f32[8,128]{1,0:T(8,128)S(1)}, u32[]{:S(2)}, u32[]{:S(2)}) collective-permute-start(f32[8,128]{1,0:T(8,128)S(1)} %all_dots.1.refs_0_), channel_id=1, source_target_pairs={{0,2},{1,3},{2,0},{3,1},{4,6},{5,7},{6,4},{7,5},{8,10},{9,11},{10,... | collective-permute-start | bytes 12296 | tf_op jit(solution)/shard_map/ppermute | solution.py:202
  36.6 0.7 %finish.2 = f32[4,32,256]{2,1,0:T(8,128)} custom-call(f32[128,256]{1,0:T(8,128)S(1)} %get-tuple-element.25.mine, bf16[144,256]{1,0:T(8,128)(2,1)S(1)} %collective-permute-done.17.refs_0_, bf16[144,256]{1,0:T(8,128)(2,1)S(1)} %collective-permute-done.18.refs_1_, bf16[144,256]{1,0:T(8,128)(2,1)S(1)} %collective-permute-done.19.refs_2_), custom_call_target="tpu_custom_call" | custom-call | tf_op jit(solution)/shard_map/finish/pallas_call | solution.py:19
  37.3 2.4 %collective-permute-done.15.refs_1_ = bf16[128,256]{1,0:T(8,128)(2,1)S(1)} collective-permute-done((bf16[128,256]{1,0:T(8,128)(2,1)S(1)}, bf16[128,256]{1,0:T(8,128)(2,1)S(1)}, u32[]{:S(2)}, u32[]{:S(2)}) %collective-permute-start.15) | collective-permute-done | bytes 65568 | tf_op jit(solution)/shard_map/ppermute | solution.py:202
  39.6 0.7 %finish.3 = f32[4,32,256]{2,1,0:T(8,128)} custom-call(f32[128,256]{1,0:T(8,128)S(1)} %get-tuple-element.30.mine, bf16[128,256]{1,0:T(8,128)(2,1)S(1)} %collective-permute-done.14.refs_0_, bf16[128,256]{1,0:T(8,128)(2,1)S(1)} %collective-permute-done.15.refs_1_, bf16[128,256]{1,0:T(8,128)(2,1)S(1)} %collective-permute-done.16.refs_2_), custom_call_target="tpu_custom_call" | custom-call | tf_op jit(solution)/shard_map/finish/pallas_call | solution.py:19
  40.4 0.6 %subspace.1 = f32[2,2]{1,0:T(2,128)} custom-call(f32[8,128]{1,0:T(8,128)S(1)} %all_dots.1.refs_0_, f32[8,128]{1,0:T(8,128)S(1)} %collective-permute-done.20.refs_1_, f32[8,128]{1,0:T(8,128)S(1)} %collective-permute-done.21.refs_2_, f32[8,128]{1,0:T(8,128)S(1)} %collective-permute-done.22.refs_3_), custom_call_target="tpu_custom_call" | custom-call | tf_op jit(solution)/shard_map/subspace/pallas_call | solution.py:19
  (35 shorter events, 0.2 us)
Async XLA Ops:
  0.6 8.1 %collective-permute-start.1 = (bf16[4,32,256]{2,1,0:T(8,128)(2,1)}, bf16[4,32,256]{2,1,0:T(8,128)(2,1)S(1)}, u32[]{:S(2)}, u32[]{:S(2)}) collective-permute-start(bf16[4,32,256]{2,1,0:T(8,128)(2,1)} %refs_0_.1), channel_id=1, source_target_pairs={{0,8},{4,12},{8,0},{12,4},{1,9},{5,13},{9,1},{13,5},{2,10},{6,14},... | collective-permute-start | bytes 196616 | tf_op jit(solution)/shard_map/ppermute | solution.py:202
  4.7 6.2 %collective-permute-start.3 = (bf16[4,32,256]{2,1,0:T(8,128)(2,1)}, bf16[4,32,256]{2,1,0:T(8,128)(2,1)S(1)}, u32[]{:S(2)}, u32[]{:S(2)}) collective-permute-start(bf16[4,32,256]{2,1,0:T(8,128)(2,1)} %refs_0_.1), channel_id=1, source_target_pairs={{0,1},{1,0},{2,3},{3,2},{4,5},{5,4},{6,7},{7,6},{8,9},{9,8},{10,11... | collective-permute-start | bytes 196616 | tf_op jit(solution)/shard_map/ppermute | solution.py:202
  4.7 7.0 %collective-permute-start.8 = (bf16[4,32,256]{2,1,0:T(8,128)(2,1)}, bf16[4,32,256]{2,1,0:T(8,128)(2,1)S(1)}, u32[]{:S(2)}, u32[]{:S(2)}) collective-permute-start(bf16[4,32,256]{2,1,0:T(8,128)(2,1)} %refs_8_.1), channel_id=1, source_target_pairs={{0,8},{4,12},{8,0},{12,4},{1,9},{5,13},{9,1},{13,5},{2,10},{6,14},... | collective-permute-start | bytes 196616 | tf_op jit(solution)/shard_map/ppermute | solution.py:202
  4.9 7.2 %collective-permute-start.10 = (bf16[4,32,256]{2,1,0:T(8,128)(2,1)}, bf16[4,32,256]{2,1,0:T(8,128)(2,1)S(1)}, u32[]{:S(2)}, u32[]{:S(2)}) collective-permute-start(bf16[4,32,256]{2,1,0:T(8,128)(2,1)} %refs_8_.1), channel_id=1, source_target_pairs={{0,1},{1,0},{2,3},{3,2},{4,5},{5,4},{6,7},{7,6},{8,9},{9,8},{10,11... | collective-permute-start | bytes 196616 | tf_op jit(solution)/shard_map/ppermute | solution.py:202
  5.2 1.1 %copy-start = (bf16[4,32,256]{2,1,0:T(8,128)(2,1)S(1)}, bf16[4,32,256]{2,1,0:T(8,128)(2,1)}, u32[]{:S(2)}) copy-start(bf16[4,32,256]{2,1,0:T(8,128)(2,1)} %refs_0_.1) | copy-start | bytes 196612
  5.2 3.5 %copy-start.1 = (bf16[4,32,256]{2,1,0:T(8,128)(2,1)S(1)}, bf16[4,32,256]{2,1,0:T(8,128)(2,1)}, u32[]{:S(2)}) copy-start(bf16[4,32,256]{2,1,0:T(8,128)(2,1)} %refs_8_.1) | copy-start | bytes 196612
  6.4 8.9 %collective-permute-start = (bf16[4,32,256]{2,1,0:T(8,128)(2,1)S(1)}, bf16[4,32,256]{2,1,0:T(8,128)(2,1)S(1)}, u32[]{:S(2)}, u32[]{:S(2)}) collective-permute-start(bf16[4,32,256]{2,1,0:T(8,128)(2,1)S(1)} %copy-done), channel_id=1, source_target_pairs={{0,4},{4,0},{8,12},{12,8},{1,5},{5,1},{9,13},{13,9},{2,6},{6,2},{1... | collective-permute-start | bytes 196616 | tf_op jit(solution)/shard_map/ppermute | solution.py:202
  8.7 5.1 %copy-start.2 = (s32[1,1,64]{2,1,0:T(1,128)S(1)}, s32[1,1,64]{2,1,0:T(1,128)}, u32[]{:S(2)}) copy-start(s32[1,1,64]{2,1,0:T(1,128)} %param.15) | copy-start | bytes 772
  8.8 5.1 %copy-start.3 = (s32[1,1,64]{2,1,0:T(1,128)S(1)}, s32[1,1,64]{2,1,0:T(1,128)}, u32[]{:S(2)}) copy-start(s32[1,1,64]{2,1,0:T(1,128)} %param.13) | copy-start | bytes 772
  8.8 6.6 %collective-permute-start.7 = (bf16[4,32,256]{2,1,0:T(8,128)(2,1)S(1)}, bf16[4,32,256]{2,1,0:T(8,128)(2,1)S(1)}, u32[]{:S(2)}, u32[]{:S(2)}) collective-permute-start(bf16[4,32,256]{2,1,0:T(8,128)(2,1)S(1)} %copy-done.1), channel_id=1, source_target_pairs={{0,4},{4,0},{8,12},{12,8},{1,5},{5,1},{9,13},{13,9},{2,6},{6,2},{1... | collective-permute-start | bytes 196616 | tf_op jit(solution)/shard_map/ppermute | solution.py:202
  10.9 5.0 %collective-permute-start.5 = (bf16[4,32,256]{2,1,0:T(8,128)(2,1)S(1)}, bf16[4,32,256]{2,1,0:T(8,128)(2,1)S(1)}, u32[]{:S(2)}, u32[]{:S(2)}) collective-permute-start(bf16[4,32,256]{2,1,0:T(8,128)(2,1)S(1)} %collective-permute-done.1.refs_2_), channel_id=1, source_target_pairs={{0,1},{1,0},{2,3},{3,2},{4,5},{5,4},{6,7},{7,6},{8,9},{9,8},{10,11... | collective-permute-start | bytes 196616 | tf_op jit(solution)/shard_map/ppermute | solution.py:202
  11.8 4.4 %collective-permute-start.2 = (bf16[4,32,256]{2,1,0:T(8,128)(2,1)S(1)}, bf16[4,32,256]{2,1,0:T(8,128)(2,1)S(1)}, u32[]{:S(2)}, u32[]{:S(2)}) collective-permute-start(bf16[4,32,256]{2,1,0:T(8,128)(2,1)S(1)} %collective-permute-done.1.refs_2_), channel_id=1, source_target_pairs={{0,4},{4,0},{8,12},{12,8},{1,5},{5,1},{9,13},{13,9},{2,6},{6,2},{1... | collective-permute-start | bytes 196616 | tf_op jit(solution)/shard_map/ppermute | solution.py:202
  12.1 4.7 %collective-permute-start.9 = (bf16[4,32,256]{2,1,0:T(8,128)(2,1)S(1)}, bf16[4,32,256]{2,1,0:T(8,128)(2,1)S(1)}, u32[]{:S(2)}, u32[]{:S(2)}) collective-permute-start(bf16[4,32,256]{2,1,0:T(8,128)(2,1)S(1)} %collective-permute-done.8.refs_10_), channel_id=1, source_target_pairs={{0,4},{4,0},{8,12},{12,8},{1,5},{5,1},{9,13},{13,9},{2,6},{6,2},{1... | collective-permute-start | bytes 196616 | tf_op jit(solution)/shard_map/ppermute | solution.py:202
  15.3 2.2 %collective-permute-start.12 = (bf16[4,32,256]{2,1,0:T(8,128)(2,1)S(1)}, bf16[4,32,256]{2,1,0:T(8,128)(2,1)S(1)}, u32[]{:S(2)}, u32[]{:S(2)}) collective-permute-start(bf16[4,32,256]{2,1,0:T(8,128)(2,1)S(1)} %collective-permute-done.8.refs_10_), channel_id=1, source_target_pairs={{0,1},{1,0},{2,3},{3,2},{4,5},{5,4},{6,7},{7,6},{8,9},{9,8},{10,11... | collective-permute-start | bytes 196616 | tf_op jit(solution)/shard_map/ppermute | solution.py:202
  15.4 2.1 %collective-permute-start.4 = (bf16[4,32,256]{2,1,0:T(8,128)(2,1)S(1)}, bf16[4,32,256]{2,1,0:T(8,128)(2,1)S(1)}, u32[]{:S(2)}, u32[]{:S(2)}) collective-permute-start(bf16[4,32,256]{2,1,0:T(8,128)(2,1)S(1)} %collective-permute-done.refs_1_), channel_id=1, source_target_pairs={{0,1},{1,0},{2,3},{3,2},{4,5},{5,4},{6,7},{7,6},{8,9},{9,8},{10,11... | collective-permute-start | bytes 196616 | tf_op jit(solution)/shard_map/ppermute | solution.py:202
  15.9 1.7 %collective-permute-start.11 = (bf16[4,32,256]{2,1,0:T(8,128)(2,1)S(1)}, bf16[4,32,256]{2,1,0:T(8,128)(2,1)S(1)}, u32[]{:S(2)}, u32[]{:S(2)}) collective-permute-start(bf16[4,32,256]{2,1,0:T(8,128)(2,1)S(1)} %collective-permute-done.7.refs_9_), channel_id=1, source_target_pairs={{0,1},{1,0},{2,3},{3,2},{4,5},{5,4},{6,7},{7,6},{8,9},{9,8},{10,11... | collective-permute-start | bytes 196616 | tf_op jit(solution)/shard_map/ppermute | solution.py:202
  16.1 1.4 %collective-permute-start.6 = (bf16[4,32,256]{2,1,0:T(8,128)(2,1)S(1)}, bf16[4,32,256]{2,1,0:T(8,128)(2,1)S(1)}, u32[]{:S(2)}, u32[]{:S(2)}) collective-permute-start(bf16[4,32,256]{2,1,0:T(8,128)(2,1)S(1)} %collective-permute-done.2.refs_3_), channel_id=1, source_target_pairs={{0,1},{1,0},{2,3},{3,2},{4,5},{5,4},{6,7},{7,6},{8,9},{9,8},{10,11... | collective-permute-start | bytes 196616 | tf_op jit(solution)/shard_map/ppermute | solution.py:202
  16.8 1.3 %collective-permute-start.13 = (bf16[4,32,256]{2,1,0:T(8,128)(2,1)S(1)}, bf16[4,32,256]{2,1,0:T(8,128)(2,1)S(1)}, u32[]{:S(2)}, u32[]{:S(2)}) collective-permute-start(bf16[4,32,256]{2,1,0:T(8,128)(2,1)S(1)} %collective-permute-done.9.refs_11_), channel_id=1, source_target_pairs={{0,1},{1,0},{2,3},{3,2},{4,5},{5,4},{6,7},{7,6},{8,9},{9,8},{10,11... | collective-permute-start | bytes 196616 | tf_op jit(solution)/shard_map/ppermute | solution.py:202
  16.9 0.7 %copy-start.4 = (s32[1,1,64]{2,1,0:T(1,128)S(1)}, s32[1,1,64]{2,1,0:T(1,128)}, u32[]{:S(2)}) copy-start(s32[1,1,64]{2,1,0:T(1,128)} %param.14) | copy-start | bytes 772
  16.9 0.7 %copy-start.5 = (s32[1,1,64]{2,1,0:T(1,128)S(1)}, s32[1,1,64]{2,1,0:T(1,128)}, u32[]{:S(2)}) copy-start(s32[1,1,64]{2,1,0:T(1,128)} %param.16) | copy-start | bytes 772
  21.1 10.5 %collective-permute-start.17 = (bf16[144,256]{1,0:T(8,128)(2,1)S(1)}, bf16[144,256]{1,0:T(8,128)(2,1)S(1)}, u32[]{:S(2)}, u32[]{:S(2)}) collective-permute-start(bf16[144,256]{1,0:T(8,128)(2,1)S(1)} %get-tuple-element.26), channel_id=1, source_target_pairs={{0,4},{4,0},{8,12},{12,8},{1,5},{5,1},{9,13},{13,9},{2,6},{6,2},{1... | collective-permute-start | bytes 221192 | tf_op jit(solution)/shard_map/ppermute | solution.py:202
  24.7 8.0 %collective-permute-start.18 = (bf16[144,256]{1,0:T(8,128)(2,1)S(1)}, bf16[144,256]{1,0:T(8,128)(2,1)S(1)}, u32[]{:S(2)}, u32[]{:S(2)}) collective-permute-start(bf16[144,256]{1,0:T(8,128)(2,1)S(1)} %get-tuple-element.27), channel_id=1, source_target_pairs={{0,8},{4,12},{8,0},{12,4},{1,9},{5,13},{9,1},{13,5},{2,10},{6,14},... | collective-permute-start | bytes 221192 | tf_op jit(solution)/shard_map/ppermute | solution.py:202
  27.2 7.3 %collective-permute-start.19 = (bf16[144,256]{1,0:T(8,128)(2,1)S(1)}, bf16[144,256]{1,0:T(8,128)(2,1)S(1)}, u32[]{:S(2)}, u32[]{:S(2)}) collective-permute-start(bf16[144,256]{1,0:T(8,128)(2,1)S(1)} %get-tuple-element.28), channel_id=1, source_target_pairs={{0,12},{4,8},{8,4},{12,0},{1,13},{5,9},{9,5},{13,1},{2,14},{6,10},... | collective-permute-start | bytes 221192 | tf_op jit(solution)/shard_map/ppermute | solution.py:202
  28.3 8.2 %collective-permute-start.14 = (bf16[128,256]{1,0:T(8,128)(2,1)S(1)}, bf16[128,256]{1,0:T(8,128)(2,1)S(1)}, u32[]{:S(2)}, u32[]{:S(2)}) collective-permute-start(bf16[128,256]{1,0:T(8,128)(2,1)S(1)} %get-tuple-element.22), channel_id=1, source_target_pairs={{0,4},{4,0},{8,12},{12,8},{1,5},{5,1},{9,13},{13,9},{2,6},{6,2},{1... | collective-permute-start | bytes 196616 | tf_op jit(solution)/shard_map/ppermute | solution.py:202
  28.9 10.8 %collective-permute-start.15 = (bf16[128,256]{1,0:T(8,128)(2,1)S(1)}, bf16[128,256]{1,0:T(8,128)(2,1)S(1)}, u32[]{:S(2)}, u32[]{:S(2)}) collective-permute-start(bf16[128,256]{1,0:T(8,128)(2,1)S(1)} %get-tuple-element.23), channel_id=1, source_target_pairs={{0,8},{4,12},{8,0},{12,4},{1,9},{5,13},{9,1},{13,5},{2,10},{6,14},... | collective-permute-start | bytes 196616 | tf_op jit(solution)/shard_map/ppermute | solution.py:202
  31.6 8.1 %collective-permute-start.16 = (bf16[128,256]{1,0:T(8,128)(2,1)S(1)}, bf16[128,256]{1,0:T(8,128)(2,1)S(1)}, u32[]{:S(2)}, u32[]{:S(2)}) collective-permute-start(bf16[128,256]{1,0:T(8,128)(2,1)S(1)} %get-tuple-element.24), channel_id=1, source_target_pairs={{0,12},{4,8},{8,4},{12,0},{1,13},{5,9},{9,5},{13,1},{2,14},{6,10},... | collective-permute-start | bytes 196616 | tf_op jit(solution)/shard_map/ppermute | solution.py:202
  34.6 5.8 %collective-permute-start.22 = (f32[8,128]{1,0:T(8,128)S(1)}, f32[8,128]{1,0:T(8,128)S(1)}, u32[]{:S(2)}, u32[]{:S(2)}) collective-permute-start(f32[8,128]{1,0:T(8,128)S(1)} %all_dots.1.refs_0_), channel_id=1, source_target_pairs={{0,3},{1,2},{2,1},{3,0},{4,7},{5,6},{6,5},{7,4},{8,11},{9,10},{10,... | collective-permute-start | bytes 12296 | tf_op jit(solution)/shard_map/ppermute | solution.py:202
  34.6 5.7 %collective-permute-start.21 = (f32[8,128]{1,0:T(8,128)S(1)}, f32[8,128]{1,0:T(8,128)S(1)}, u32[]{:S(2)}, u32[]{:S(2)}) collective-permute-start(f32[8,128]{1,0:T(8,128)S(1)} %all_dots.1.refs_0_), channel_id=1, source_target_pairs={{0,2},{1,3},{2,0},{3,1},{4,6},{5,7},{6,4},{7,5},{8,10},{9,11},{10,... | collective-permute-start | bytes 12296 | tf_op jit(solution)/shard_map/ppermute | solution.py:202
  36.5 3.8 %collective-permute-start.20 = (f32[8,128]{1,0:T(8,128)S(1)}, f32[8,128]{1,0:T(8,128)S(1)}, u32[]{:S(2)}, u32[]{:S(2)}) collective-permute-start(f32[8,128]{1,0:T(8,128)S(1)} %all_dots.1.refs_0_), channel_id=1, source_target_pairs={{0,1},{1,0},{2,3},{3,2},{4,5},{5,4},{6,7},{7,6},{8,9},{9,8},{10,11... | collective-permute-start | bytes 12296 | tf_op jit(solution)/shard_map/ppermute | solution.py:202
where the time goes:
time: 41.4 us; the launch traced here: 40.9 us
  starting transfers between devices  25 us (60%)
  waiting for transfers between devices  6.21 us (15%)
  Pallas kernels  4.98 us (12%)
  local copies, waits for them, and re-layouts  2.17 us (5%)
  between operations  1.43 us (3%)
  other arithmetic  1.14 us (3%)
    ppermute x23, starting transfers between devices, swap(): return lax.ppermute(x, axes, [(i, i ^ hop) for i in range(size)])  25 us
    ppermute x23, waiting for transfers between devices, swap(): return lax.ppermute(x, axes, [(i, i ^ hop) for i in range(size)])  6.21 us
    pallas_call x5, Pallas kernels, call(): pl.pallas_call(kernel, out_shape=outs, in_specs=[SCALARS] * n_scalars + [...  4.98 us
    unnamed x13, local copies, waits for them, and re-layouts  2.17 us
    select_n x1, other arithmetic, local(): left = jnp.take(lefts, helper, axis=2)  1.13 us
  transfers between devices with their start and end apart: 23, of which 6 were waited for; matrix products, arithmetic and copies ran while one was open for 6% of the time, Pallas kernels for 3%

commit v1 on v0

--- a/solution.py
+++ b/solution.py
@@ -48,27 +48,22 @@
                 for w in range(2):
                     part = tile_of(wave * parts[w])
                     dots[v][w] = part if dots[v][w] is None else dots[v][w] + part
-    row = lax.broadcasted_iota(jnp.int32, (8, 128), 0)
-    lane = lax.broadcasted_iota(jnp.int32, (8, 128), 1)
-    tile = jnp.zeros((8, 128), F32)
-    for v in range(2):
-        for w in range(2):
-            tile = jnp.where((row == v) & (lane == w), jnp.sum(dots[v][w]), tile)
-    return tile
+    rows = [jnp.sum(dots[v][w], axis=0, keepdims=True) for v in range(2) for w in range(2)]
+    return jnp.concatenate(rows + [jnp.zeros((4, 128), F32)])
 
 
 def to_wire(tile, width):
     high = tile.astype(BF16).astype(F32)
     middle = (tile - high).astype(BF16).astype(F32)
     low = tile - high - middle
-    parts = jnp.concatenate([high[:2], middle[:2], low[:2], jnp.zeros((10, 128), F32)])
+    parts = jnp.concatenate([high[:4], middle[:4], low[:4], jnp.zeros((4, 128), F32)])
     return jnp.concatenate([parts] * (width // 128), axis=1).astype(BF16)
 
 
 def from_wire(ref, at):
     parts = ref[at:, :128].astype(F32)
-    two = parts[0:2] + parts[2:4] + parts[4:6]
-    return jnp.concatenate([two, jnp.zeros((6, 128), F32)])
+    four = parts[0:4] + parts[4:8] + parts[8:12]
+    return jnp.concatenate([four, jnp.zeros((4, 128), F32)])
 
 
 def add_tasks(batch, table, left_ref, right_ref, waves, inner, sums):
@@ -106,10 +101,13 @@
                 waves[v, :, pl.ds(at, rows), :] = waves_in[v * 8 + other * 4 + k][...]
     add_tasks(batch, table, left_ref, right_ref, waves, inner, sums)
     n = sums.shape[0] * rows
-    for v in range(2):
-        for k in range(4):
-            part = sums[:, v, me ^ k].reshape(n, -1)
-            outs[4 * v + k][:n] = part if k == 0 else part.astype(BF16)
+    for k in range(4):
+        part = sums[:, 0, me ^ k].reshape(n, -1)
+        outs[k][:n] = part if k == 0 else part.astype(BF16)
+    for i, k in enumerate((0, 2)):
+        outs[4 + i][...] = sums[:, 1, me ^ k].reshape(n, -1)
+    for i, k in enumerate((1, 3)):
+        outs[6][i * n : (i + 1) * n] = sums[:, 1, me ^ k].reshape(n, -1).astype(BF16)
     tile = dots_of(me, (waves_in[:4], waves_in[8:12]), sums)
     dots_ref[...] = tile
     wire = to_wire(tile, sums.shape[-1])
@@ -120,11 +118,10 @@
 def fast_products(batch, table, left, right, waves):
     ops, n_op, rows, width = left.shape
     sectors = waves[0].shape[0]
-    outs = []
-    for v in range(2):
-        n = sectors * rows
-        outs.append(jax.ShapeDtypeStruct((n, width), F32))
-        outs += [jax.ShapeDtypeStruct((n + (16 if v == 0 else 0), width), BF16)] * 3
+    n = sectors * rows
+    own = jax.ShapeDtypeStruct((n, width), F32)
+    outs = [own] + [jax.ShapeDtypeStruct((n + 16, width), BF16)] * 3
+    outs += [own, own, jax.ShapeDtypeStruct((2 * n, width), BF16)]
     outs.append(jax.ShapeDtypeStruct((8, 128), F32))
     scratch = [
         pltpu.VMEM((2, sectors, width, width), BF16),
@@ -154,6 +151,16 @@
     return terms[0]
 
 
+def pair_kernel(cross, received, out):
+    n = cross.shape[0]
+    out[...] = (cross[...] + received[n:].astype(F32)).astype(BF16)
+
+
+def pair_sums(cross, received):
+    out = jax.ShapeDtypeStruct(cross.shape, BF16)
+    return call(pair_kernel, out, [cross, received], 0, 2, "pair_sums")
+
+
 def dots_kernel(n, own, *refs):
     refs[-1][...] = add_up([own[...]] + [from_wire(r, n) for r in refs[:-1]])
 
@@ -163,27 +170,31 @@
     return call(kernel, jax.ShapeDtypeStruct((8, 128), F32), [own, *received], 0, 1, "all_dots")
 
 
-def finish_kernel(mine, *refs):
-    received, out = refs[:-1], refs[-1]
-    n = mine.shape[0]
+def finish_kernel(scale, n, mine, *refs):
+    received, terms = refs[:n], refs[n:]
+    out = terms[-1] if scale is None else terms[-2]
+    rows = mine.shape[0]
     total = mine[...]
     for part in received:
-        total = total + part[:n].astype(F32)
+        total = total + part[:rows].astype(F32)
     out[...] = total.reshape(out.shape)
-
-
-def finish(shape, mine, received):
-    out = jax.ShapeDtypeStruct(shape, F32)
-    return call(finish_kernel, out, [mine, *received], 0, 4, "finish")
-
-
-def subspace_kernel(scale, *refs):
-    refs[-1][...] = add_up([t[:2, :2] for t in refs[:-1]]) * scale
-
-
-def subspace_of(scale, terms):
-    out = jax.ShapeDtypeStruct((2, 2), F32)
-    return call(functools.partial(subspace_kernel, scale), out, terms, 0, 1, "subspace")
+    if scale is not None:
+        write_matrix(terms[-1], add_up([t[...] for t in terms[:-2]]), scale)
+
+
+def write_matrix(out, tile, scale):
+    whole = jnp.sum(tile, axis=1, keepdims=True) * scale
+    for v in range(2):
+        for w in range(2):
+            out[v : v + 1, w : w + 1] = whole[2 * v + w : 2 * v + w + 1]
+
+
+def finish(shape, mine, received, terms=(), scale=None):
+    outs = [jax.ShapeDtypeStruct(shape, F32)]
+    if terms:
+        outs.append(jax.ShapeDtypeStruct((2, 2), F32))
+    kernel = functools.partial(finish_kernel, scale, len(received))
+    return call(kernel, outs, [mine, *received, *terms], 0, 4, "finish")
 
 
 def terms_of(x, axes):
@@ -211,18 +222,19 @@
     psi = (psi_one, psi_two)
     waves = []
     far = [swap(x, op, 2) for x in psi]
-    later, left = after(psi, left)
-    near = [[psi[v], swap(later[v], op, 1), far[v], swap(far[v], op, 1)] for v in range(2)]
+    near = [[psi[v], swap(psi[v], op, 1), far[v], swap(far[v], op, 1)] for v in range(2)]
     for v in range(2):
         waves += near[v] + [swap(x, core, 1) for x in near[v]]
     *parts, dots = fast_products(batch, table, left, right, waves)
+    paired = swap(parts[6], op, 1)
     first = [swap(x, op, k + 1) for k, x in enumerate(parts[1:4])]
-    second = [swap(x, op, k + 1) for k, x in enumerate(parts[5:8])]
+    paired, first[2] = after(paired, first[2])
+    far_sum = swap(pair_sums(parts[5], paired), op, 2)
     terms = terms_of(all_dots(dots, first), ("sec", "help"))
-    sigma_one = finish(psi_one.shape, parts[0], first)
-    second, sigma_one = after(second, sigma_one)
-    sigma_two = finish(psi_two.shape, parts[4], second)
-    return sigma_one, sigma_two, subspace_of(scale, terms)
+    (sigma_one,) = finish(psi_one.shape, parts[0], first)
+    far_sum, sigma_one = after(far_sum, sigma_one)
+    sigma_two, subspace = finish(psi_two.shape, parts[4], [paired, far_sum], terms, scale)
+    return sigma_one, sigma_two, subspace
 
 
 def general(psi_one, psi_two, left, right, table, batch, scale):
@@ -269,7 +281,7 @@
     lefts = left_blocks.reshape(ops, n_op, 2, rows, width)
     left = jnp.take(lefts, helper, axis=2)
     right = jnp.swapaxes(right_blocks, 1, 2)
-    batch = math.gcd(slots, 16)
+    batch = math.gcd(slots, 32)
     scale = 1.0 / math.sqrt(sectors * lax.axis_size("sec") * width * width)
     way = fast if n_op == 4 and rows % 16 == 0 else general
     return way(psi_one, psi_two, left, right, table, batch, scale)

time: 41.4 us -> 39.1 us (0.944)
  starting transfers between devices: 25 us -> 17.5 us
  waiting for transfers between devices: 6.21 us -> 11.8 us
  other arithmetic: 1.14 us -> 0.08 us
  local copies, waits for them, and re-layouts: 2.17 us -> 2.91 us
    ppermute x23 -> x22, starting transfers between devices: 25 us -> 17.5 us  [swap(): return lax.ppermute(x, axes, [(i, i ^ hop) for i in range(size)])]
    ppermute x23 -> x22, waiting for transfers between devices: 6.21 us -> 11.8 us  [swap(): return lax.ppermute(x, axes, [(i, i ^ hop) for i in range(size)])]
    select_n x1, other arithmetic: 1.13 us -> 0.06 us  [local(): left = jnp.take(lefts, helper, axis=2)]
    unnamed x13 -> x15, local copies, waits for them, and re-layouts: 2.17 us -> 2.91 us
  transfers between devices with their start and end apart: 23 -> 22, of which waited for: 6 -> 6; matrix products, arithmetic and copies ran while one was open for 6% -> 4% of each run, Pallas kernels for 3% -> 2%
where the time goes in v1:
time: 39.1 us; the launch traced here: 38.6 us
  starting transfers between devices  17.5 us (45%)
  waiting for transfers between devices  11.8 us (30%)
  Pallas kernels  4.93 us (13%)
  local copies, waits for them, and re-layouts  2.91 us (7%)
  between operations  1.42 us (4%)
    ppermute x22, starting transfers between devices, swap(): return lax.ppermute(x, axes, [(i, i ^ hop) for i in range(size)])  17.5 us
    ppermute x22, waiting for transfers between devices, swap(): return lax.ppermute(x, axes, [(i, i ^ hop) for i in range(size)])  11.8 us
    pallas_call x5, Pallas kernels, call(): pl.pallas_call(kernel, out_shape=outs, in_specs=[SCALARS] * n_scalars + [...  4.93 us
    unnamed x15, local copies, waits for them, and re-layouts  2.91 us
  transfers between devices with their start and end apart: 22, of which 6 were waited for; matrix products, arithmetic and copies ran while one was open for 4% of the time, Pallas kernels for 2%

profile of v1, /device:TPU:0, one launch (start us, length us, event | category | flops | bytes accessed | tf_op | source)
XLA Modules:
  0.0 38.6 jit_solution(4678145676168985372)
XLA Ops:
  0.6 4.1 %collective-permute-start.1 = (bf16[4,32,256]{2,1,0:T(8,128)(2,1)}, bf16[4,32,256]{2,1,0:T(8,128)(2,1)S(1)}, u32[]{:S(2)}, u32[]{:S(2)}) collective-permute-start(bf16[4,32,256]{2,1,0:T(8,128)(2,1)} %refs_0_.1), channel_id=1, source_target_pairs={{0,8},{4,12},{8,0},{12,4},{1,9},{5,13},{9,1},{13,5},{2,10},{6,14},... | collective-permute-start | bytes 196616 | tf_op jit(solution)/shard_map/ppermute | solution.py:213
  4.7 1.6 %collective-permute-start = (bf16[4,32,256]{2,1,0:T(8,128)(2,1)}, bf16[4,32,256]{2,1,0:T(8,128)(2,1)S(1)}, u32[]{:S(2)}, u32[]{:S(2)}) collective-permute-start(bf16[4,32,256]{2,1,0:T(8,128)(2,1)} %refs_0_.1), channel_id=1, source_target_pairs={{0,4},{4,0},{8,12},{12,8},{1,5},{5,1},{9,13},{13,9},{2,6},{6,2},{1... | collective-permute-start | bytes 196616 | tf_op jit(solution)/shard_map/ppermute | solution.py:213
  6.3 0.3 collective-permute-start.8
  6.6 0.2 collective-permute-start.7
  7.5 0.6 %copy-done.3 = s32[1,1,64]{2,1,0:T(1,128)S(1)} copy-done((s32[1,1,64]{2,1,0:T(1,128)S(1)}, s32[1,1,64]{2,1,0:T(1,128)}, u32[]{:S(2)}) %copy-start.3) | copy-done | bytes 280
  8.2 0.0 copy-done.4
  8.2 1.6 %copy.14 = bf16[8,256,256]{1,2,0:T(8,128)(2,1)S(1)} copy(bf16[8,256,256]{2,1,0:T(8,128)(2,1)} %param.12) | data formatting | bytes 2097152 | tf_op args[3]
  9.8 0.2 collective-permute-start.10
  10.0 0.3 collective-permute-start.5
  10.4 1.8 %collective-permute-start.2 = (bf16[4,32,256]{2,1,0:T(8,128)(2,1)S(1)}, bf16[4,32,256]{2,1,0:T(8,128)(2,1)S(1)}, u32[]{:S(2)}, u32[]{:S(2)}) collective-permute-start(bf16[4,32,256]{2,1,0:T(8,128)(2,1)S(1)} %collective-permute-done.1.refs_2_), channel_id=1, source_target_pairs={{0,4},{4,0},{8,12},{12,8},{1,5},{5,1},{9,13},{13,9},{2,6},{6,2},{1... | collective-permute-start | bytes 196616 | tf_op jit(solution)/shard_map/ppermute | solution.py:213
  12.2 1.0 %collective-permute-done.8.refs_10_ = bf16[4,32,256]{2,1,0:T(8,128)(2,1)S(1)} collective-permute-done((bf16[4,32,256]{2,1,0:T(8,128)(2,1)}, bf16[4,32,256]{2,1,0:T(8,128)(2,1)S(1)}, u32[]{:S(2)}, u32[]{:S(2)}) %collective-permute-start.8) | collective-permute-done | bytes 65568 | tf_op jit(solution)/shard_map/ppermute | solution.py:213
  13.2 0.1 fusion.left_ref
  13.3 0.1 collective-permute-start.12
  13.4 0.4 %collective-permute-start.4 = (bf16[4,32,256]{2,1,0:T(8,128)(2,1)S(1)}, bf16[4,32,256]{2,1,0:T(8,128)(2,1)S(1)}, u32[]{:S(2)}, u32[]{:S(2)}) collective-permute-start(bf16[4,32,256]{2,1,0:T(8,128)(2,1)S(1)} %collective-permute-done.refs_1_), channel_id=1, source_target_pairs={{0,1},{1,0},{2,3},{3,2},{4,5},{5,4},{6,7},{7,6},{8,9},{9,8},{10,11... | collective-permute-start | bytes 196616 | tf_op jit(solution)/shard_map/ppermute | solution.py:213
  13.9 0.1 collective-permute-start.11
  14.0 0.6 %collective-permute-done.2.refs_3_ = bf16[4,32,256]{2,1,0:T(8,128)(2,1)S(1)} collective-permute-done((bf16[4,32,256]{2,1,0:T(8,128)(2,1)S(1)}, bf16[4,32,256]{2,1,0:T(8,128)(2,1)S(1)}, u32[]{:S(2)}, u32[]{:S(2)}) %collective-permute-start.2) | collective-permute-done | bytes 65568 | tf_op jit(solution)/shard_map/ppermute | solution.py:213
  14.6 2.9 %collective-permute-done.9.refs_11_ = bf16[4,32,256]{2,1,0:T(8,128)(2,1)S(1)} collective-permute-done((bf16[4,32,256]{2,1,0:T(8,128)(2,1)S(1)}, bf16[4,32,256]{2,1,0:T(8,128)(2,1)S(1)}, u32[]{:S(2)}, u32[]{:S(2)}) %collective-permute-start.9) | collective-permute-done | bytes 65568 | tf_op jit(solution)/shard_map/ppermute | solution.py:213
  17.5 0.7 %copy-done.5 = s32[1,1,64]{2,1,0:T(1,128)S(1)} copy-done((s32[1,1,64]{2,1,0:T(1,128)S(1)}, s32[1,1,64]{2,1,0:T(1,128)}, u32[]{:S(2)}) %copy-start.5) | copy-done | bytes 280
  18.2 0.5 %collective-permute-done.13.refs_15_ = bf16[4,32,256]{2,1,0:T(8,128)(2,1)S(1)} collective-permute-done((bf16[4,32,256]{2,1,0:T(8,128)(2,1)S(1)}, bf16[4,32,256]{2,1,0:T(8,128)(2,1)S(1)}, u32[]{:S(2)}, u32[]{:S(2)}) %collective-permute-start.13) | collective-permute-done | bytes 65568 | tf_op jit(solution)/shard_map/ppermute | solution.py:213
  18.7 3.5 %products.1 = (f32[128,256]{1,0:T(8,128)S(1)}, bf16[144,256]{1,0:T(8,128)(2,1)S(1)}, bf16[144,256]{1,0:T(8,128)(2,1)S(1)}, bf16[144,256]{1,0:T(8,128)(2,1)S(1)},...) custom-call(s32[4,64]{1,0:T(4,128)S(1)} %pad_add_fusion.table, ...), custom_call_target="tpu_custom_call" | custom-call | tf_op jit(solution)/shard_map/products/pallas_call | solution.py:19
  22.3 0.4 %collective-permute-start.14 = (bf16[256,256]{1,0:T(8,128)(2,1)S(1)}, bf16[256,256]{1,0:T(8,128)(2,1)S(1)}, u32[]{:S(2)}, u32[]{:S(2)}) collective-permute-start(bf16[256,256]{1,0:T(8,128)(2,1)S(1)} %get-tuple-element.18), channel_id=1, source_target_pairs={{0,4},{4,0},{8,12},{12,8},{1,5},{5,1},{9,13},{13,9},{2,6},{6,2},{1... | collective-permute-start | bytes 393224 | tf_op jit(solution)/shard_map/ppermute | solution.py:213
  22.7 4.0 %collective-permute-start.15 = (bf16[144,256]{1,0:T(8,128)(2,1)S(1)}, bf16[144,256]{1,0:T(8,128)(2,1)S(1)}, u32[]{:S(2)}, u32[]{:S(2)}) collective-permute-start(bf16[144,256]{1,0:T(8,128)(2,1)S(1)} %get-tuple-element.19), channel_id=1, source_target_pairs={{0,12},{4,8},{8,4},{12,0},{1,13},{5,9},{9,5},{13,1},{2,14},{6,10},... | collective-permute-start | bytes 221192 | tf_op jit(solution)/shard_map/ppermute | solution.py:213
  26.7 0.3 collective-permute-start.17
  27.0 0.3 collective-permute-start.18
  27.3 5.4 %collective-permute-done.15.refs_2_ = bf16[144,256]{1,0:T(8,128)(2,1)S(1)} collective-permute-done((bf16[144,256]{1,0:T(8,128)(2,1)S(1)}, bf16[144,256]{1,0:T(8,128)(2,1)S(1)}, u32[]{:S(2)}, u32[]{:S(2)}) %collective-permute-start.15) | collective-permute-done | bytes 73760 | tf_op jit(solution)/shard_map/ppermute | solution.py:213
  32.7 1.2 %collective-permute-start.16 = (bf16[128,256]{1,0:T(8,128)(2,1)S(1)}, bf16[128,256]{1,0:T(8,128)(2,1)S(1)}, u32[]{:S(2)}, u32[]{:S(2)}) collective-permute-start(bf16[128,256]{1,0:T(8,128)(2,1)S(1)} %pair_sums.1), channel_id=1, source_target_pairs={{0,8},{4,12},{8,0},{12,4},{1,9},{5,13},{9,1},{13,5},{2,10},{6,14},... | collective-permute-start | bytes 196616 | tf_op jit(solution)/shard_map/ppermute | solution.py:213
  33.9 0.1 collective-permute-start.21
  34.0 1.6 %collective-permute-start.20 = (f32[8,128]{1,0:T(8,128)S(1)}, f32[8,128]{1,0:T(8,128)S(1)}, u32[]{:S(2)}, u32[]{:S(2)}) collective-permute-start(f32[8,128]{1,0:T(8,128)S(1)} %all_dots.1.refs_2_), channel_id=1, source_target_pairs={{0,2},{1,3},{2,0},{3,1},{4,6},{5,7},{6,4},{7,5},{8,10},{9,11},{10,... | collective-permute-start | bytes 12296 | tf_op jit(solution)/shard_map/ppermute | solution.py:213
  35.6 0.3 collective-permute-start.19
  35.9 0.7 %finish.2 = f32[4,32,256]{2,1,0:T(8,128)} custom-call(f32[128,256]{1,0:T(8,128)S(1)} %get-tuple-element.21.mine, bf16[144,256]{1,0:T(8,128)(2,1)S(1)} %collective-permute-done.17.refs_0_, bf16[144,256]{1,0:T(8,128)(2,1)S(1)} %collective-permute-done.18.refs_1_, bf16[144,256]{1,0:T(8,128)(2,1)S(1)} %collective-permute-done.15.refs_2_), custom_call_target="tpu_custom_call" | custom-call | tf_op jit(solution)/shard_map/finish/pallas_call | solution.py:19
  36.6 1.4 %collective-permute-done.16.refs_1_ = bf16[128,256]{1,0:T(8,128)(2,1)S(1)} collective-permute-done((bf16[128,256]{1,0:T(8,128)(2,1)S(1)}, bf16[128,256]{1,0:T(8,128)(2,1)S(1)}, u32[]{:S(2)}, u32[]{:S(2)}) %collective-permute-start.16) | collective-permute-done | bytes 65568 | tf_op jit(solution)/shard_map/ppermute | solution.py:213
  37.9 0.7 %finish.3 = (f32[4,32,256]{2,1,0:T(8,128)}, f32[2,2]{1,0:T(2,128)}) custom-call(f32[128,256]{1,0:T(8,128)S(1)} %get-tuple-element.26.mine, bf16[256,256]{1,0:T(8,128)(2,1)S(1)} %collective-permute-done.14.received.refs_0_, bf16[128,256]{1,0:T(8,128)(2,1)S(1)} %collective-permute-done.16.refs_1_, f32[8,128]{1,0:T(8,128)S(1)} %all_dots.1.refs_2_, ...), custom_call_target="tpu_custom_call" | custom-call | tf_op jit(solution)/shard_map/finish/pallas_call | solution.py:19
  (35 shorter events, 0.1 us)
Async XLA Ops:
  0.6 9.1 %collective-permute-start.1 = (bf16[4,32,256]{2,1,0:T(8,128)(2,1)}, bf16[4,32,256]{2,1,0:T(8,128)(2,1)S(1)}, u32[]{:S(2)}, u32[]{:S(2)}) collective-permute-start(bf16[4,32,256]{2,1,0:T(8,128)(2,1)} %refs_0_.1), channel_id=1, source_target_pairs={{0,8},{4,12},{8,0},{12,4},{1,9},{5,13},{9,1},{13,5},{2,10},{6,14},... | collective-permute-start | bytes 196616 | tf_op jit(solution)/shard_map/ppermute | solution.py:213
  4.7 5.3 %collective-permute-start = (bf16[4,32,256]{2,1,0:T(8,128)(2,1)}, bf16[4,32,256]{2,1,0:T(8,128)(2,1)S(1)}, u32[]{:S(2)}, u32[]{:S(2)}) collective-permute-start(bf16[4,32,256]{2,1,0:T(8,128)(2,1)} %refs_0_.1), channel_id=1, source_target_pairs={{0,4},{4,0},{8,12},{12,8},{1,5},{5,1},{9,13},{13,9},{2,6},{6,2},{1... | collective-permute-start | bytes 196616 | tf_op jit(solution)/shard_map/ppermute | solution.py:213
  6.3 4.1 %collective-permute-start.3 = (bf16[4,32,256]{2,1,0:T(8,128)(2,1)}, bf16[4,32,256]{2,1,0:T(8,128)(2,1)S(1)}, u32[]{:S(2)}, u32[]{:S(2)}) collective-permute-start(bf16[4,32,256]{2,1,0:T(8,128)(2,1)} %refs_0_.1), channel_id=1, source_target_pairs={{0,1},{1,0},{2,3},{3,2},{4,5},{5,4},{6,7},{7,6},{8,9},{9,8},{10,11... | collective-permute-start | bytes 196616 | tf_op jit(solution)/shard_map/ppermute | solution.py:213
  6.3 6.9 %collective-permute-start.8 = (bf16[4,32,256]{2,1,0:T(8,128)(2,1)}, bf16[4,32,256]{2,1,0:T(8,128)(2,1)S(1)}, u32[]{:S(2)}, u32[]{:S(2)}) collective-permute-start(bf16[4,32,256]{2,1,0:T(8,128)(2,1)} %refs_8_.1), channel_id=1, source_target_pairs={{0,8},{4,12},{8,0},{12,4},{1,9},{5,13},{9,1},{13,5},{2,10},{6,14},... | collective-permute-start | bytes 196616 | tf_op jit(solution)/shard_map/ppermute | solution.py:213
  6.6 6.7 %collective-permute-start.7 = (bf16[4,32,256]{2,1,0:T(8,128)(2,1)}, bf16[4,32,256]{2,1,0:T(8,128)(2,1)S(1)}, u32[]{:S(2)}, u32[]{:S(2)}) collective-permute-start(bf16[4,32,256]{2,1,0:T(8,128)(2,1)} %refs_8_.1), channel_id=1, source_target_pairs={{0,4},{4,0},{8,12},{12,8},{1,5},{5,1},{9,13},{13,9},{2,6},{6,2},{1... | collective-permute-start | bytes 196616 | tf_op jit(solution)/shard_map/ppermute | solution.py:213
  7.5 0.7 %copy-start.3 = (s32[1,1,64]{2,1,0:T(1,128)S(1)}, s32[1,1,64]{2,1,0:T(1,128)}, u32[]{:S(2)}) copy-start(s32[1,1,64]{2,1,0:T(1,128)} %param.15) | copy-start | bytes 772
  7.5 0.7 %copy-start.4 = (s32[1,1,64]{2,1,0:T(1,128)S(1)}, s32[1,1,64]{2,1,0:T(1,128)}, u32[]{:S(2)}) copy-start(s32[1,1,64]{2,1,0:T(1,128)} %param.13) | copy-start | bytes 772
  8.2 1.6 %copy-start.1 = (bf16[4,32,256]{2,1,0:T(8,128)(2,1)S(1)}, bf16[4,32,256]{2,1,0:T(8,128)(2,1)}, u32[]{:S(2)}) copy-start(bf16[4,32,256]{2,1,0:T(8,128)(2,1)} %refs_8_.1) | copy-start | bytes 196612
  8.2 5.1 %copy-start.2 = (bf16[8,256,256]{2,1,0:T(8,128)(2,1)S(1)}, bf16[8,256,256]{2,1,0:T(8,128)(2,1)}, u32[]{:S(2)}) copy-start(bf16[8,256,256]{2,1,0:T(8,128)(2,1)} %param.11) | copy-start | bytes 3145732
  9.8 3.7 %collective-permute-start.10 = (bf16[4,32,256]{2,1,0:T(8,128)(2,1)S(1)}, bf16[4,32,256]{2,1,0:T(8,128)(2,1)S(1)}, u32[]{:S(2)}, u32[]{:S(2)}) collective-permute-start(bf16[4,32,256]{2,1,0:T(8,128)(2,1)S(1)} %copy-done.1), channel_id=1, source_target_pairs={{0,1},{1,0},{2,3},{3,2},{4,5},{5,4},{6,7},{7,6},{8,9},{9,8},{10,11... | collective-permute-start | bytes 196616 | tf_op jit(solution)/shard_map/ppermute | solution.py:213
  10.0 3.9 %collective-permute-start.5 = (bf16[4,32,256]{2,1,0:T(8,128)(2,1)S(1)}, bf16[4,32,256]{2,1,0:T(8,128)(2,1)S(1)}, u32[]{:S(2)}, u32[]{:S(2)}) collective-permute-start(bf16[4,32,256]{2,1,0:T(8,128)(2,1)S(1)} %collective-permute-done.1.refs_2_), channel_id=1, source_target_pairs={{0,1},{1,0},{2,3},{3,2},{4,5},{5,4},{6,7},{7,6},{8,9},{9,8},{10,11... | collective-permute-start | bytes 196616 | tf_op jit(solution)/shard_map/ppermute | solution.py:213
  10.4 4.3 %collective-permute-start.2 = (bf16[4,32,256]{2,1,0:T(8,128)(2,1)S(1)}, bf16[4,32,256]{2,1,0:T(8,128)(2,1)S(1)}, u32[]{:S(2)}, u32[]{:S(2)}) collective-permute-start(bf16[4,32,256]{2,1,0:T(8,128)(2,1)S(1)} %collective-permute-done.1.refs_2_), channel_id=1, source_target_pairs={{0,4},{4,0},{8,12},{12,8},{1,5},{5,1},{9,13},{13,9},{2,6},{6,2},{1... | collective-permute-start | bytes 196616 | tf_op jit(solution)/shard_map/ppermute | solution.py:213
  13.2 4.3 %collective-permute-start.9 = (bf16[4,32,256]{2,1,0:T(8,128)(2,1)S(1)}, bf16[4,32,256]{2,1,0:T(8,128)(2,1)S(1)}, u32[]{:S(2)}, u32[]{:S(2)}) collective-permute-start(bf16[4,32,256]{2,1,0:T(8,128)(2,1)S(1)} %collective-permute-done.8.refs_10_), channel_id=1, source_target_pairs={{0,4},{4,0},{8,12},{12,8},{1,5},{5,1},{9,13},{13,9},{2,6},{6,2},{1... | collective-permute-start | bytes 196616 | tf_op jit(solution)/shard_map/ppermute | solution.py:213
  13.2 5.5 %copy-start = (bf16[4,32,256]{2,1,0:T(8,128)(2,1)S(1)}, bf16[4,32,256]{2,1,0:T(8,128)(2,1)}, u32[]{:S(2)}) copy-start(bf16[4,32,256]{2,1,0:T(8,128)(2,1)} %refs_0_.1) | copy-start | bytes 196612
  13.3 4.9 %collective-permute-start.12 = (bf16[4,32,256]{2,1,0:T(8,128)(2,1)S(1)}, bf16[4,32,256]{2,1,0:T(8,128)(2,1)S(1)}, u32[]{:S(2)}, u32[]{:S(2)}) collective-permute-start(bf16[4,32,256]{2,1,0:T(8,128)(2,1)S(1)} %collective-permute-done.8.refs_10_), channel_id=1, source_target_pairs={{0,1},{1,0},{2,3},{3,2},{4,5},{5,4},{6,7},{7,6},{8,9},{9,8},{10,11... | collective-permute-start | bytes 196616 | tf_op jit(solution)/shard_map/ppermute | solution.py:213
  13.4 4.7 %collective-permute-start.4 = (bf16[4,32,256]{2,1,0:T(8,128)(2,1)S(1)}, bf16[4,32,256]{2,1,0:T(8,128)(2,1)S(1)}, u32[]{:S(2)}, u32[]{:S(2)}) collective-permute-start(bf16[4,32,256]{2,1,0:T(8,128)(2,1)S(1)} %collective-permute-done.refs_1_), channel_id=1, source_target_pairs={{0,1},{1,0},{2,3},{3,2},{4,5},{5,4},{6,7},{7,6},{8,9},{9,8},{10,11... | collective-permute-start | bytes 196616 | tf_op jit(solution)/shard_map/ppermute | solution.py:213
  13.9 4.3 %collective-permute-start.11 = (bf16[4,32,256]{2,1,0:T(8,128)(2,1)S(1)}, bf16[4,32,256]{2,1,0:T(8,128)(2,1)S(1)}, u32[]{:S(2)}, u32[]{:S(2)}) collective-permute-start(bf16[4,32,256]{2,1,0:T(8,128)(2,1)S(1)} %collective-permute-done.7.refs_9_), channel_id=1, source_target_pairs={{0,1},{1,0},{2,3},{3,2},{4,5},{5,4},{6,7},{7,6},{8,9},{9,8},{10,11... | collective-permute-start | bytes 196616 | tf_op jit(solution)/shard_map/ppermute | solution.py:213
  14.6 3.6 %collective-permute-start.6 = (bf16[4,32,256]{2,1,0:T(8,128)(2,1)S(1)}, bf16[4,32,256]{2,1,0:T(8,128)(2,1)S(1)}, u32[]{:S(2)}, u32[]{:S(2)}) collective-permute-start(bf16[4,32,256]{2,1,0:T(8,128)(2,1)S(1)} %collective-permute-done.2.refs_3_), channel_id=1, source_target_pairs={{0,1},{1,0},{2,3},{3,2},{4,5},{5,4},{6,7},{7,6},{8,9},{9,8},{10,11... | collective-permute-start | bytes 196616 | tf_op jit(solution)/shard_map/ppermute | solution.py:213
  17.5 1.3 %collective-permute-start.13 = (bf16[4,32,256]{2,1,0:T(8,128)(2,1)S(1)}, bf16[4,32,256]{2,1,0:T(8,128)(2,1)S(1)}, u32[]{:S(2)}, u32[]{:S(2)}) collective-permute-start(bf16[4,32,256]{2,1,0:T(8,128)(2,1)S(1)} %collective-permute-done.9.refs_11_), channel_id=1, source_target_pairs={{0,1},{1,0},{2,3},{3,2},{4,5},{5,4},{6,7},{7,6},{8,9},{9,8},{10,11... | collective-permute-start | bytes 196616 | tf_op jit(solution)/shard_map/ppermute | solution.py:213
  17.5 0.7 %copy-start.5 = (s32[1,1,64]{2,1,0:T(1,128)S(1)}, s32[1,1,64]{2,1,0:T(1,128)}, u32[]{:S(2)}) copy-start(s32[1,1,64]{2,1,0:T(1,128)} %param.14) | copy-start | bytes 772
  17.5 0.7 %copy-start.6 = (s32[1,1,64]{2,1,0:T(1,128)S(1)}, s32[1,1,64]{2,1,0:T(1,128)}, u32[]{:S(2)}) copy-start(s32[1,1,64]{2,1,0:T(1,128)} %param.16) | copy-start | bytes 772
  22.3 10.4 %collective-permute-start.14 = (bf16[256,256]{1,0:T(8,128)(2,1)S(1)}, bf16[256,256]{1,0:T(8,128)(2,1)S(1)}, u32[]{:S(2)}, u32[]{:S(2)}) collective-permute-start(bf16[256,256]{1,0:T(8,128)(2,1)S(1)} %get-tuple-element.18), channel_id=1, source_target_pairs={{0,4},{4,0},{8,12},{12,8},{1,5},{5,1},{9,13},{13,9},{2,6},{6,2},{1... | collective-permute-start | bytes 393224 | tf_op jit(solution)/shard_map/ppermute | solution.py:213
  22.7 10.0 %collective-permute-start.15 = (bf16[144,256]{1,0:T(8,128)(2,1)S(1)}, bf16[144,256]{1,0:T(8,128)(2,1)S(1)}, u32[]{:S(2)}, u32[]{:S(2)}) collective-permute-start(bf16[144,256]{1,0:T(8,128)(2,1)S(1)} %get-tuple-element.19), channel_id=1, source_target_pairs={{0,12},{4,8},{8,4},{12,0},{1,13},{5,9},{9,5},{13,1},{2,14},{6,10},... | collective-permute-start | bytes 221192 | tf_op jit(solution)/shard_map/ppermute | solution.py:213
  26.7 7.2 %collective-permute-start.17 = (bf16[144,256]{1,0:T(8,128)(2,1)S(1)}, bf16[144,256]{1,0:T(8,128)(2,1)S(1)}, u32[]{:S(2)}, u32[]{:S(2)}) collective-permute-start(bf16[144,256]{1,0:T(8,128)(2,1)S(1)} %get-tuple-element.22), channel_id=1, source_target_pairs={{0,4},{4,0},{8,12},{12,8},{1,5},{5,1},{9,13},{13,9},{2,6},{6,2},{1... | collective-permute-start | bytes 221192 | tf_op jit(solution)/shard_map/ppermute | solution.py:213
  27.0 6.9 %collective-permute-start.18 = (bf16[144,256]{1,0:T(8,128)(2,1)S(1)}, bf16[144,256]{1,0:T(8,128)(2,1)S(1)}, u32[]{:S(2)}, u32[]{:S(2)}) collective-permute-start(bf16[144,256]{1,0:T(8,128)(2,1)S(1)} %get-tuple-element.23), channel_id=1, source_target_pairs={{0,8},{4,12},{8,0},{12,4},{1,9},{5,13},{9,1},{13,5},{2,10},{6,14},... | collective-permute-start | bytes 221192 | tf_op jit(solution)/shard_map/ppermute | solution.py:213
  32.7 5.2 %collective-permute-start.16 = (bf16[128,256]{1,0:T(8,128)(2,1)S(1)}, bf16[128,256]{1,0:T(8,128)(2,1)S(1)}, u32[]{:S(2)}, u32[]{:S(2)}) collective-permute-start(bf16[128,256]{1,0:T(8,128)(2,1)S(1)} %pair_sums.1), channel_id=1, source_target_pairs={{0,8},{4,12},{8,0},{12,4},{1,9},{5,13},{9,1},{13,5},{2,10},{6,14},... | collective-permute-start | bytes 196616 | tf_op jit(solution)/shard_map/ppermute | solution.py:213
  33.9 4.0 %collective-permute-start.21 = (f32[8,128]{1,0:T(8,128)S(1)}, f32[8,128]{1,0:T(8,128)S(1)}, u32[]{:S(2)}, u32[]{:S(2)}) collective-permute-start(f32[8,128]{1,0:T(8,128)S(1)} %all_dots.1.refs_2_), channel_id=1, source_target_pairs={{0,3},{1,2},{2,1},{3,0},{4,7},{5,6},{6,5},{7,4},{8,11},{9,10},{10,... | collective-permute-start | bytes 12296 | tf_op jit(solution)/shard_map/ppermute | solution.py:213
  34.0 3.9 %collective-permute-start.20 = (f32[8,128]{1,0:T(8,128)S(1)}, f32[8,128]{1,0:T(8,128)S(1)}, u32[]{:S(2)}, u32[]{:S(2)}) collective-permute-start(f32[8,128]{1,0:T(8,128)S(1)} %all_dots.1.refs_2_), channel_id=1, source_target_pairs={{0,2},{1,3},{2,0},{3,1},{4,6},{5,7},{6,4},{7,5},{8,10},{9,11},{10,... | collective-permute-start | bytes 12296 | tf_op jit(solution)/shard_map/ppermute | solution.py:213
  35.6 2.4 %collective-permute-start.19 = (f32[8,128]{1,0:T(8,128)S(1)}, f32[8,128]{1,0:T(8,128)S(1)}, u32[]{:S(2)}, u32[]{:S(2)}) collective-permute-start(f32[8,128]{1,0:T(8,128)S(1)} %all_dots.1.refs_2_), channel_id=1, source_target_pairs={{0,1},{1,0},{2,3},{3,2},{4,5},{5,4},{6,7},{7,6},{8,9},{9,8},{10,11... | collective-permute-start | bytes 12296 | tf_op jit(solution)/shard_map/ppermute | solution.py:213

commit v2 on v1

--- a/solution.py
+++ b/solution.py
@@ -66,7 +66,7 @@
     return jnp.concatenate([four, jnp.zeros((4, 128), F32)])
 
 
-def add_tasks(batch, table, left_ref, right_ref, waves, inner, sums):
+def add_tasks(batch, table, left_ref, right_ref, waves, inner, sums, odd):
     sectors, _, n_op, rows, width = sums.shape
     ops, half = right_ref.shape[0], n_op * rows
     left = left_ref[...].reshape(ops * half, width)
@@ -76,21 +76,24 @@
             inner[pl.ds(a * ops, ops), v] = found.reshape(ops, half, width)
     inner[sectors * ops] = jnp.zeros((2, half, width), BF16)
     sums[...] = jnp.zeros_like(sums)
+    odd[...] = jnp.zeros_like(odd)
 
     def step(g, carry):
         for i in range(batch):
             t = g * batch + i
             block = inner[table[0, t]].reshape(2 * half, width)
             found = jnp.dot(block, right_ref[table[1, t]], preferred_element_type=F32)
-            sums[table[2, t]] += found.reshape(2, n_op, rows, width)
+            total = odd if i % 2 else sums
+            total[table[2, t]] += found.reshape(2, n_op, rows, width)
         return carry
 
     lax.fori_loop(0, (table[3, 2] + batch - 1) // batch, step, 0)
+    sums[...] += odd[...]
 
 
 def fast_kernel(batch, table, left_ref, right_ref, *refs):
     waves_in, refs = refs[:16], refs[16:]
-    *outs, dots_ref, waves, inner, sums = refs
+    *outs, dots_ref, waves, inner, sums, odd = refs
     rows = sums.shape[3]
     me, helper = table[3, 0], table[3, 1]
     for v in range(2):
@@ -99,7 +102,7 @@
                 owner = helper if other == 0 else 1 - helper
                 at = pl.multiple_of(((me ^ k) * 2 + owner) * rows, rows)
                 waves[v, :, pl.ds(at, rows), :] = waves_in[v * 8 + other * 4 + k][...]
-    add_tasks(batch, table, left_ref, right_ref, waves, inner, sums)
+    add_tasks(batch, table, left_ref, right_ref, waves, inner, sums, odd)
     n = sums.shape[0] * rows
     for k in range(4):
         part = sums[:, 0, me ^ k].reshape(n, -1)
@@ -127,20 +130,21 @@
         pltpu.VMEM((2, sectors, width, width), BF16),
         pltpu.VMEM((sectors * ops + 1, 2, n_op * rows, width), BF16),
         pltpu.VMEM((sectors, 2, n_op, rows, width), F32),
+        pltpu.VMEM((sectors, 2, n_op, rows, width), F32),
     ]
     kernel = functools.partial(fast_kernel, batch)
     return call(kernel, outs, [table, left, right, *waves], 1, 20, "products", scratch)
 
 
-def any_kernel(batch, table, left_ref, right_ref, waves, sums, inner):
-    add_tasks(batch, table, left_ref, right_ref, waves, inner, sums)
+def any_kernel(batch, table, left_ref, right_ref, waves, sums, inner, odd):
+    add_tasks(batch, table, left_ref, right_ref, waves, inner, sums, odd)
 
 
 def any_products(batch, table, left, right, waves):
     ops, n_op, rows, width = left.shape
     sectors = waves.shape[1]
     out = jax.ShapeDtypeStruct((sectors, 2, n_op, rows, width), F32)
-    scratch = [pltpu.VMEM((sectors * ops + 1, 2, n_op * rows, width), BF16)]
+    scratch = [pltpu.VMEM((sectors * ops + 1, 2, n_op * rows, width), BF16), pltpu.VMEM(out.shape, F32)]
     kernel = functools.partial(any_kernel, batch)
     return call(kernel, out, [table, left, right, waves], 1, 20, "products", scratch)
 
@@ -223,6 +227,9 @@
     waves = []
     far = [swap(x, op, 2) for x in psi]
     near = [[psi[v], swap(psi[v], op, 1), far[v], swap(far[v], op, 1)] for v in range(2)]
+    late, near[0][3] = after(psi, near[0][3])
+    for v in range(2):
+        near[v][0] = late[v]
     for v in range(2):
         waves += near[v] + [swap(x, core, 1) for x in near[v]]
     *parts, dots = fast_products(batch, table, left, right, waves)

time: 39.1 us -> 38.5 us (0.985)
  waiting for transfers between devices: 11.8 us -> 10.4 us
  Pallas kernels: 4.93 us -> 6.26 us
    ppermute x22, waiting for transfers between devices: 11.8 us -> 10.4 us  [swap(): return lax.ppermute(x, axes, [(i, i ^ hop) for i in range(size)])]
    pallas_call x5, Pallas kernels: 4.93 us -> 6.26 us  [call(): pl.pallas_call(kernel, out_shape=outs, in_specs=[SCALARS] * n_scalars + [...]
  transfers between devices with their start and end apart: 22 -> 22, of which waited for: 6 -> 7; matrix products, arithmetic and copies ran while one was open for 4% -> 4% of each run, Pallas kernels for 2% -> 2%
where the time goes in v2:
time: 38.5 us; the launch traced here: 38.4 us
  starting transfers between devices  17.3 us (45%)
  waiting for transfers between devices  10.4 us (27%)
  Pallas kernels  6.26 us (16%)
  local copies, waits for them, and re-layouts  2.9 us (8%)
  between operations  1.42 us (4%)
    ppermute x22, starting transfers between devices, swap(): return lax.ppermute(x, axes, [(i, i ^ hop) for i in range(size)])  17.3 us
    ppermute x22, waiting for transfers between devices, swap(): return lax.ppermute(x, axes, [(i, i ^ hop) for i in range(size)])  10.4 us
    pallas_call x5, Pallas kernels, call(): pl.pallas_call(kernel, out_shape=outs, in_specs=[SCALARS] * n_scalars + [...  6.26 us
    unnamed x15, local copies, waits for them, and re-layouts  2.9 us
  transfers between devices with their start and end apart: 22, of which 7 were waited for; matrix products, arithmetic and copies ran while one was open for 4% of the time, Pallas kernels for 2%

profile of v2, /device:TPU:0, one launch (start us, length us, event | category | flops | bytes accessed | tf_op | source)
XLA Modules:
  0.0 38.4 jit_solution(10843966339553018485)
XLA Ops:
  0.6 4.1 %collective-permute-start = (bf16[4,32,256]{2,1,0:T(8,128)(2,1)}, bf16[4,32,256]{2,1,0:T(8,128)(2,1)S(1)}, u32[]{:S(2)}, u32[]{:S(2)}) collective-permute-start(bf16[4,32,256]{2,1,0:T(8,128)(2,1)} %refs_0_), channel_id=1, source_target_pairs={{0,8},{4,12},{8,0},{12,4},{1,9},{5,13},{9,1},{13,5},{2,10},{6,14},... | collective-permute-start | bytes 196616 | tf_op jit(solution)/shard_map/ppermute | solution.py:217
  4.7 1.6 %collective-permute-start.2 = (bf16[4,32,256]{2,1,0:T(8,128)(2,1)}, bf16[4,32,256]{2,1,0:T(8,128)(2,1)S(1)}, u32[]{:S(2)}, u32[]{:S(2)}) collective-permute-start(bf16[4,32,256]{2,1,0:T(8,128)(2,1)} %refs_0_), channel_id=1, source_target_pairs={{0,4},{4,0},{8,12},{12,8},{1,5},{5,1},{9,13},{13,9},{2,6},{6,2},{1... | collective-permute-start | bytes 196616 | tf_op jit(solution)/shard_map/ppermute | solution.py:217
  6.3 0.3 collective-permute-start.8
  6.6 0.2 collective-permute-start.7
  7.5 0.6 %copy-done.3 = s32[1,1,64]{2,1,0:T(1,128)S(1)} copy-done((s32[1,1,64]{2,1,0:T(1,128)S(1)}, s32[1,1,64]{2,1,0:T(1,128)}, u32[]{:S(2)}) %copy-start.3) | copy-done | bytes 280
  8.2 1.6 %copy.14 = bf16[8,256,256]{1,2,0:T(8,128)(2,1)S(1)} copy(bf16[8,256,256]{2,1,0:T(8,128)(2,1)} %param.12) | data formatting | bytes 2097152 | tf_op args[3]
  9.8 0.1 collective-permute-start.5
  9.8 1.9 %collective-permute-start.1 = (bf16[4,32,256]{2,1,0:T(8,128)(2,1)S(1)}, bf16[4,32,256]{2,1,0:T(8,128)(2,1)S(1)}, u32[]{:S(2)}, u32[]{:S(2)}) collective-permute-start(bf16[4,32,256]{2,1,0:T(8,128)(2,1)S(1)} %collective-permute-done.refs_2_), channel_id=1, source_target_pairs={{0,4},{4,0},{8,12},{12,8},{1,5},{5,1},{9,13},{13,9},{2,6},{6,2},{1... | collective-permute-start | bytes 196616 | tf_op jit(solution)/shard_map/ppermute | solution.py:217
  11.7 0.6 %collective-permute-done.8.refs_10_ = bf16[4,32,256]{2,1,0:T(8,128)(2,1)S(1)} collective-permute-done((bf16[4,32,256]{2,1,0:T(8,128)(2,1)}, bf16[4,32,256]{2,1,0:T(8,128)(2,1)S(1)}, u32[]{:S(2)}, u32[]{:S(2)}) %collective-permute-start.8) | collective-permute-done | bytes 65568 | tf_op jit(solution)/shard_map/ppermute | solution.py:217
  12.3 0.3 collective-permute-start.9
  12.5 0.3 collective-permute-start.4
  12.9 0.1 fusion.left_ref
  12.9 1.5 %collective-permute-done.1.refs_3_ = bf16[4,32,256]{2,1,0:T(8,128)(2,1)S(1)} collective-permute-done((bf16[4,32,256]{2,1,0:T(8,128)(2,1)S(1)}, bf16[4,32,256]{2,1,0:T(8,128)(2,1)S(1)}, u32[]{:S(2)}, u32[]{:S(2)}) %collective-permute-start.1) | collective-permute-done | bytes 65568 | tf_op jit(solution)/shard_map/ppermute | solution.py:217
  14.4 0.5 %collective-permute-start.3 = (bf16[4,32,256]{2,1,0:T(8,128)(2,1)S(1)}, bf16[4,32,256]{2,1,0:T(8,128)(2,1)S(1)}, u32[]{:S(2)}, u32[]{:S(2)}) collective-permute-start(bf16[4,32,256]{2,1,0:T(8,128)(2,1)S(1)} %copy-done), channel_id=1, source_target_pairs={{0,1},{1,0},{2,3},{3,2},{4,5},{5,4},{6,7},{7,6},{8,9},{9,8},{10,11... | collective-permute-start | bytes 196616 | tf_op jit(solution)/shard_map/ppermute | solution.py:217
  14.9 0.1 collective-permute-start.6
  15.0 0.4 %collective-permute-start.10 = (bf16[4,32,256]{2,1,0:T(8,128)(2,1)S(1)}, bf16[4,32,256]{2,1,0:T(8,128)(2,1)S(1)}, u32[]{:S(2)}, u32[]{:S(2)}) collective-permute-start(bf16[4,32,256]{2,1,0:T(8,128)(2,1)S(1)} %copy-done.1), channel_id=1, source_target_pairs={{0,1},{1,0},{2,3},{3,2},{4,5},{5,4},{6,7},{7,6},{8,9},{9,8},{10,11... | collective-permute-start | bytes 196616 | tf_op jit(solution)/shard_map/ppermute | solution.py:217
  15.5 1.3 %collective-permute-done.9.refs_11_ = bf16[4,32,256]{2,1,0:T(8,128)(2,1)S(1)} collective-permute-done((bf16[4,32,256]{2,1,0:T(8,128)(2,1)S(1)}, bf16[4,32,256]{2,1,0:T(8,128)(2,1)S(1)}, u32[]{:S(2)}, u32[]{:S(2)}) %collective-permute-start.9) | collective-permute-done | bytes 65568 | tf_op jit(solution)/shard_map/ppermute | solution.py:217
  16.8 0.7 %copy-done.5 = s32[1,1,64]{2,1,0:T(1,128)S(1)} copy-done((s32[1,1,64]{2,1,0:T(1,128)S(1)}, s32[1,1,64]{2,1,0:T(1,128)}, u32[]{:S(2)}) %copy-start.5) | copy-done | bytes 280
  17.5 0.5 %collective-permute-done.13.refs_15_ = bf16[4,32,256]{2,1,0:T(8,128)(2,1)S(1)} collective-permute-done((bf16[4,32,256]{2,1,0:T(8,128)(2,1)S(1)}, bf16[4,32,256]{2,1,0:T(8,128)(2,1)S(1)}, u32[]{:S(2)}, u32[]{:S(2)}) %collective-permute-start.13) | collective-permute-done | bytes 65568 | tf_op jit(solution)/shard_map/ppermute | solution.py:217
  18.1 4.9 %products.1 = (f32[128,256]{1,0:T(8,128)S(1)}, bf16[144,256]{1,0:T(8,128)(2,1)S(1)}, bf16[144,256]{1,0:T(8,128)(2,1)S(1)}, bf16[144,256]{1,0:T(8,128)(2,1)S(1)},...) custom-call(s32[4,64]{1,0:T(4,128)S(1)} %pad_add_fusion.table, ...), custom_call_target="tpu_custom_call" | custom-call | tf_op jit(solution)/shard_map/products/pallas_call | solution.py:19
  22.9 0.9 %collective-permute-start.14 = (bf16[256,256]{1,0:T(8,128)(2,1)S(1)}, bf16[256,256]{1,0:T(8,128)(2,1)S(1)}, u32[]{:S(2)}, u32[]{:S(2)}) collective-permute-start(bf16[256,256]{1,0:T(8,128)(2,1)S(1)} %get-tuple-element.24), channel_id=1, source_target_pairs={{0,4},{4,0},{8,12},{12,8},{1,5},{5,1},{9,13},{13,9},{2,6},{6,2},{1... | collective-permute-start | bytes 393224 | tf_op jit(solution)/shard_map/ppermute | solution.py:217
  23.8 2.6 %collective-permute-start.15 = (bf16[144,256]{1,0:T(8,128)(2,1)S(1)}, bf16[144,256]{1,0:T(8,128)(2,1)S(1)}, u32[]{:S(2)}, u32[]{:S(2)}) collective-permute-start(bf16[144,256]{1,0:T(8,128)(2,1)S(1)} %get-tuple-element.25), channel_id=1, source_target_pairs={{0,12},{4,8},{8,4},{12,0},{1,13},{5,9},{9,5},{13,1},{2,14},{6,10},... | collective-permute-start | bytes 221192 | tf_op jit(solution)/shard_map/ppermute | solution.py:217
  26.5 1.8 %collective-permute-start.18 = (bf16[144,256]{1,0:T(8,128)(2,1)S(1)}, bf16[144,256]{1,0:T(8,128)(2,1)S(1)}, u32[]{:S(2)}, u32[]{:S(2)}) collective-permute-start(bf16[144,256]{1,0:T(8,128)(2,1)S(1)} %get-tuple-element.29), channel_id=1, source_target_pairs={{0,8},{4,12},{8,0},{12,4},{1,9},{5,13},{9,1},{13,5},{2,10},{6,14},... | collective-permute-start | bytes 221192 | tf_op jit(solution)/shard_map/ppermute | solution.py:217
  28.2 4.2 %collective-permute-done.15.refs_2_ = bf16[144,256]{1,0:T(8,128)(2,1)S(1)} collective-permute-done((bf16[144,256]{1,0:T(8,128)(2,1)S(1)}, bf16[144,256]{1,0:T(8,128)(2,1)S(1)}, u32[]{:S(2)}, u32[]{:S(2)}) %collective-permute-start.15) | collective-permute-done | bytes 73760 | tf_op jit(solution)/shard_map/ppermute | solution.py:217
  32.5 0.1 collective-permute-start.16
  32.5 0.9 %collective-permute-done.17.refs_0_ = bf16[144,256]{1,0:T(8,128)(2,1)S(1)} collective-permute-done((bf16[144,256]{1,0:T(8,128)(2,1)S(1)}, bf16[144,256]{1,0:T(8,128)(2,1)S(1)}, u32[]{:S(2)}, u32[]{:S(2)}) %collective-permute-start.17) | collective-permute-done | bytes 73760 | tf_op jit(solution)/shard_map/ppermute | solution.py:217
  33.4 0.1 collective-permute-start.21
  33.5 2.0 %collective-permute-start.20 = (f32[8,128]{1,0:T(8,128)S(1)}, f32[8,128]{1,0:T(8,128)S(1)}, u32[]{:S(2)}, u32[]{:S(2)}) collective-permute-start(f32[8,128]{1,0:T(8,128)S(1)} %all_dots.1.refs_2_), channel_id=1, source_target_pairs={{0,2},{1,3},{2,0},{3,1},{4,6},{5,7},{6,4},{7,5},{8,10},{9,11},{10,... | collective-permute-start | bytes 12296 | tf_op jit(solution)/shard_map/ppermute | solution.py:217
  35.5 0.0 collective-permute-start.19
  35.6 0.7 %finish.2 = f32[4,32,256]{2,1,0:T(8,128)} custom-call(f32[128,256]{1,0:T(8,128)S(1)} %get-tuple-element.27.mine, bf16[144,256]{1,0:T(8,128)(2,1)S(1)} %collective-permute-done.17.refs_0_, bf16[144,256]{1,0:T(8,128)(2,1)S(1)} %collective-permute-done.18.refs_1_, bf16[144,256]{1,0:T(8,128)(2,1)S(1)} %collective-permute-done.15.refs_2_), custom_call_target="tpu_custom_call" | custom-call | tf_op jit(solution)/shard_map/finish/pallas_call | solution.py:19
  36.3 1.4 %collective-permute-done.16.refs_1_ = bf16[128,256]{1,0:T(8,128)(2,1)S(1)} collective-permute-done((bf16[128,256]{1,0:T(8,128)(2,1)S(1)}, bf16[128,256]{1,0:T(8,128)(2,1)S(1)}, u32[]{:S(2)}, u32[]{:S(2)}) %collective-permute-start.16) | collective-permute-done | bytes 65568 | tf_op jit(solution)/shard_map/ppermute | solution.py:217
  37.7 0.7 %finish.3 = (f32[4,32,256]{2,1,0:T(8,128)}, f32[2,2]{1,0:T(2,128)}) custom-call(f32[128,256]{1,0:T(8,128)S(1)} %get-tuple-element.32.mine, bf16[256,256]{1,0:T(8,128)(2,1)S(1)} %collective-permute-done.14.received.refs_0_, bf16[128,256]{1,0:T(8,128)(2,1)S(1)} %collective-permute-done.16.refs_1_, f32[8,128]{1,0:T(8,128)S(1)} %all_dots.1.refs_2_, ...), custom_call_target="tpu_custom_call" | custom-call | tf_op jit(solution)/shard_map/finish/pallas_call | solution.py:19
  (35 shorter events, 0.1 us)
Async XLA Ops:
  0.6 9.1 %collective-permute-start = (bf16[4,32,256]{2,1,0:T(8,128)(2,1)}, bf16[4,32,256]{2,1,0:T(8,128)(2,1)S(1)}, u32[]{:S(2)}, u32[]{:S(2)}) collective-permute-start(bf16[4,32,256]{2,1,0:T(8,128)(2,1)} %refs_0_), channel_id=1, source_target_pairs={{0,8},{4,12},{8,0},{12,4},{1,9},{5,13},{9,1},{13,5},{2,10},{6,14},... | collective-permute-start | bytes 196616 | tf_op jit(solution)/shard_map/ppermute | solution.py:217
  4.7 7.6 %collective-permute-start.2 = (bf16[4,32,256]{2,1,0:T(8,128)(2,1)}, bf16[4,32,256]{2,1,0:T(8,128)(2,1)S(1)}, u32[]{:S(2)}, u32[]{:S(2)}) collective-permute-start(bf16[4,32,256]{2,1,0:T(8,128)(2,1)} %refs_0_), channel_id=1, source_target_pairs={{0,4},{4,0},{8,12},{12,8},{1,5},{5,1},{9,13},{13,9},{2,6},{6,2},{1... | collective-permute-start | bytes 196616 | tf_op jit(solution)/shard_map/ppermute | solution.py:217
  6.3 6.0 %collective-permute-start.8 = (bf16[4,32,256]{2,1,0:T(8,128)(2,1)}, bf16[4,32,256]{2,1,0:T(8,128)(2,1)S(1)}, u32[]{:S(2)}, u32[]{:S(2)}) collective-permute-start(bf16[4,32,256]{2,1,0:T(8,128)(2,1)} %refs_8_), channel_id=1, source_target_pairs={{0,8},{4,12},{8,0},{12,4},{1,9},{5,13},{9,1},{13,5},{2,10},{6,14},... | collective-permute-start | bytes 196616 | tf_op jit(solution)/shard_map/ppermute | solution.py:217
  6.6 5.9 %collective-permute-start.7 = (bf16[4,32,256]{2,1,0:T(8,128)(2,1)}, bf16[4,32,256]{2,1,0:T(8,128)(2,1)S(1)}, u32[]{:S(2)}, u32[]{:S(2)}) collective-permute-start(bf16[4,32,256]{2,1,0:T(8,128)(2,1)} %refs_8_), channel_id=1, source_target_pairs={{0,4},{4,0},{8,12},{12,8},{1,5},{5,1},{9,13},{13,9},{2,6},{6,2},{1... | collective-permute-start | bytes 196616 | tf_op jit(solution)/shard_map/ppermute | solution.py:217
  7.5 0.7 %copy-start.3 = (s32[1,1,64]{2,1,0:T(1,128)S(1)}, s32[1,1,64]{2,1,0:T(1,128)}, u32[]{:S(2)}) copy-start(s32[1,1,64]{2,1,0:T(1,128)} %param.15) | copy-start | bytes 772
  7.5 0.7 %copy-start.4 = (s32[1,1,64]{2,1,0:T(1,128)S(1)}, s32[1,1,64]{2,1,0:T(1,128)}, u32[]{:S(2)}) copy-start(s32[1,1,64]{2,1,0:T(1,128)} %param.13) | copy-start | bytes 772
  8.2 4.7 %copy-start.2 = (bf16[8,256,256]{2,1,0:T(8,128)(2,1)S(1)}, bf16[8,256,256]{2,1,0:T(8,128)(2,1)}, u32[]{:S(2)}) copy-start(bf16[8,256,256]{2,1,0:T(8,128)(2,1)} %param.11) | copy-start | bytes 3145732
  9.8 4.7 %collective-permute-start.5 = (bf16[4,32,256]{2,1,0:T(8,128)(2,1)S(1)}, bf16[4,32,256]{2,1,0:T(8,128)(2,1)S(1)}, u32[]{:S(2)}, u32[]{:S(2)}) collective-permute-start(bf16[4,32,256]{2,1,0:T(8,128)(2,1)S(1)} %collective-permute-done.refs_2_), channel_id=1, source_target_pairs={{0,1},{1,0},{2,3},{3,2},{4,5},{5,4},{6,7},{7,6},{8,9},{9,8},{10,11... | collective-permute-start | bytes 196616 | tf_op jit(solution)/shard_map/ppermute | solution.py:217
  9.8 4.6 %collective-permute-start.1 = (bf16[4,32,256]{2,1,0:T(8,128)(2,1)S(1)}, bf16[4,32,256]{2,1,0:T(8,128)(2,1)S(1)}, u32[]{:S(2)}, u32[]{:S(2)}) collective-permute-start(bf16[4,32,256]{2,1,0:T(8,128)(2,1)S(1)} %collective-permute-done.refs_2_), channel_id=1, source_target_pairs={{0,4},{4,0},{8,12},{12,8},{1,5},{5,1},{9,13},{13,9},{2,6},{6,2},{1... | collective-permute-start | bytes 196616 | tf_op jit(solution)/shard_map/ppermute | solution.py:217
  12.3 2.7 %collective-permute-start.12 = (bf16[4,32,256]{2,1,0:T(8,128)(2,1)S(1)}, bf16[4,32,256]{2,1,0:T(8,128)(2,1)S(1)}, u32[]{:S(2)}, u32[]{:S(2)}) collective-permute-start(bf16[4,32,256]{2,1,0:T(8,128)(2,1)S(1)} %collective-permute-done.8.refs_10_), channel_id=1, source_target_pairs={{0,1},{1,0},{2,3},{3,2},{4,5},{5,4},{6,7},{7,6},{8,9},{9,8},{10,11... | collective-permute-start | bytes 196616 | tf_op jit(solution)/shard_map/ppermute | solution.py:217
  12.3 4.5 %collective-permute-start.9 = (bf16[4,32,256]{2,1,0:T(8,128)(2,1)S(1)}, bf16[4,32,256]{2,1,0:T(8,128)(2,1)S(1)}, u32[]{:S(2)}, u32[]{:S(2)}) collective-permute-start(bf16[4,32,256]{2,1,0:T(8,128)(2,1)S(1)} %collective-permute-done.8.refs_10_), channel_id=1, source_target_pairs={{0,4},{4,0},{8,12},{12,8},{1,5},{5,1},{9,13},{13,9},{2,6},{6,2},{1... | collective-permute-start | bytes 196616 | tf_op jit(solution)/shard_map/ppermute | solution.py:217
  12.5 2.4 %collective-permute-start.4 = (bf16[4,32,256]{2,1,0:T(8,128)(2,1)S(1)}, bf16[4,32,256]{2,1,0:T(8,128)(2,1)S(1)}, u32[]{:S(2)}, u32[]{:S(2)}) collective-permute-start(bf16[4,32,256]{2,1,0:T(8,128)(2,1)S(1)} %collective-permute-done.2.refs_1_), channel_id=1, source_target_pairs={{0,1},{1,0},{2,3},{3,2},{4,5},{5,4},{6,7},{7,6},{8,9},{9,8},{10,11... | collective-permute-start | bytes 196616 | tf_op jit(solution)/shard_map/ppermute | solution.py:217
  12.9 1.6 %copy-start = (bf16[4,32,256]{2,1,0:T(8,128)(2,1)S(1)}, bf16[4,32,256]{2,1,0:T(8,128)(2,1)}, u32[]{:S(2)}) copy-start(bf16[4,32,256]{2,1,0:T(8,128)(2,1)} %refs_0_) | copy-start | bytes 196612
  12.9 2.1 %copy-start.1 = (bf16[4,32,256]{2,1,0:T(8,128)(2,1)S(1)}, bf16[4,32,256]{2,1,0:T(8,128)(2,1)}, u32[]{:S(2)}) copy-start(bf16[4,32,256]{2,1,0:T(8,128)(2,1)} %refs_8_) | copy-start | bytes 196612
  14.4 3.1 %collective-permute-start.11 = (bf16[4,32,256]{2,1,0:T(8,128)(2,1)S(1)}, bf16[4,32,256]{2,1,0:T(8,128)(2,1)S(1)}, u32[]{:S(2)}, u32[]{:S(2)}) collective-permute-start(bf16[4,32,256]{2,1,0:T(8,128)(2,1)S(1)} %collective-permute-done.7.refs_9_), channel_id=1, source_target_pairs={{0,1},{1,0},{2,3},{3,2},{4,5},{5,4},{6,7},{7,6},{8,9},{9,8},{10,11... | collective-permute-start | bytes 196616 | tf_op jit(solution)/shard_map/ppermute | solution.py:217
  14.4 3.1 %collective-permute-start.3 = (bf16[4,32,256]{2,1,0:T(8,128)(2,1)S(1)}, bf16[4,32,256]{2,1,0:T(8,128)(2,1)S(1)}, u32[]{:S(2)}, u32[]{:S(2)}) collective-permute-start(bf16[4,32,256]{2,1,0:T(8,128)(2,1)S(1)} %copy-done), channel_id=1, source_target_pairs={{0,1},{1,0},{2,3},{3,2},{4,5},{5,4},{6,7},{7,6},{8,9},{9,8},{10,11... | collective-permute-start | bytes 196616 | tf_op jit(solution)/shard_map/ppermute | solution.py:217
  14.9 2.6 %collective-permute-start.6 = (bf16[4,32,256]{2,1,0:T(8,128)(2,1)S(1)}, bf16[4,32,256]{2,1,0:T(8,128)(2,1)S(1)}, u32[]{:S(2)}, u32[]{:S(2)}) collective-permute-start(bf16[4,32,256]{2,1,0:T(8,128)(2,1)S(1)} %collective-permute-done.1.refs_3_), channel_id=1, source_target_pairs={{0,1},{1,0},{2,3},{3,2},{4,5},{5,4},{6,7},{7,6},{8,9},{9,8},{10,11... | collective-permute-start | bytes 196616 | tf_op jit(solution)/shard_map/ppermute | solution.py:217
  15.0 2.5 %collective-permute-start.10 = (bf16[4,32,256]{2,1,0:T(8,128)(2,1)S(1)}, bf16[4,32,256]{2,1,0:T(8,128)(2,1)S(1)}, u32[]{:S(2)}, u32[]{:S(2)}) collective-permute-start(bf16[4,32,256]{2,1,0:T(8,128)(2,1)S(1)} %copy-done.1), channel_id=1, source_target_pairs={{0,1},{1,0},{2,3},{3,2},{4,5},{5,4},{6,7},{7,6},{8,9},{9,8},{10,11... | collective-permute-start | bytes 196616 | tf_op jit(solution)/shard_map/ppermute | solution.py:217
  16.8 1.3 %collective-permute-start.13 = (bf16[4,32,256]{2,1,0:T(8,128)(2,1)S(1)}, bf16[4,32,256]{2,1,0:T(8,128)(2,1)S(1)}, u32[]{:S(2)}, u32[]{:S(2)}) collective-permute-start(bf16[4,32,256]{2,1,0:T(8,128)(2,1)S(1)} %collective-permute-done.9.refs_11_), channel_id=1, source_target_pairs={{0,1},{1,0},{2,3},{3,2},{4,5},{5,4},{6,7},{7,6},{8,9},{9,8},{10,11... | collective-permute-start | bytes 196616 | tf_op jit(solution)/shard_map/ppermute | solution.py:217
  16.8 0.7 %copy-start.5 = (s32[1,1,64]{2,1,0:T(1,128)S(1)}, s32[1,1,64]{2,1,0:T(1,128)}, u32[]{:S(2)}) copy-start(s32[1,1,64]{2,1,0:T(1,128)} %param.14) | copy-start | bytes 772
  16.8 0.7 %copy-start.6 = (s32[1,1,64]{2,1,0:T(1,128)S(1)}, s32[1,1,64]{2,1,0:T(1,128)}, u32[]{:S(2)}) copy-start(s32[1,1,64]{2,1,0:T(1,128)} %param.16) | copy-start | bytes 772
  22.9 9.5 %collective-permute-start.14 = (bf16[256,256]{1,0:T(8,128)(2,1)S(1)}, bf16[256,256]{1,0:T(8,128)(2,1)S(1)}, u32[]{:S(2)}, u32[]{:S(2)}) collective-permute-start(bf16[256,256]{1,0:T(8,128)(2,1)S(1)} %get-tuple-element.24), channel_id=1, source_target_pairs={{0,4},{4,0},{8,12},{12,8},{1,5},{5,1},{9,13},{13,9},{2,6},{6,2},{1... | collective-permute-start | bytes 393224 | tf_op jit(solution)/shard_map/ppermute | solution.py:217
  23.8 8.6 %collective-permute-start.15 = (bf16[144,256]{1,0:T(8,128)(2,1)S(1)}, bf16[144,256]{1,0:T(8,128)(2,1)S(1)}, u32[]{:S(2)}, u32[]{:S(2)}) collective-permute-start(bf16[144,256]{1,0:T(8,128)(2,1)S(1)} %get-tuple-element.25), channel_id=1, source_target_pairs={{0,12},{4,8},{8,4},{12,0},{1,13},{5,9},{9,5},{13,1},{2,14},{6,10},... | collective-permute-start | bytes 221192 | tf_op jit(solution)/shard_map/ppermute | solution.py:217
  26.5 6.9 %collective-permute-start.17 = (bf16[144,256]{1,0:T(8,128)(2,1)S(1)}, bf16[144,256]{1,0:T(8,128)(2,1)S(1)}, u32[]{:S(2)}, u32[]{:S(2)}) collective-permute-start(bf16[144,256]{1,0:T(8,128)(2,1)S(1)} %get-tuple-element.28), channel_id=1, source_target_pairs={{0,4},{4,0},{8,12},{12,8},{1,5},{5,1},{9,13},{13,9},{2,6},{6,2},{1... | collective-permute-start | bytes 221192 | tf_op jit(solution)/shard_map/ppermute | solution.py:217
  26.5 6.9 %collective-permute-start.18 = (bf16[144,256]{1,0:T(8,128)(2,1)S(1)}, bf16[144,256]{1,0:T(8,128)(2,1)S(1)}, u32[]{:S(2)}, u32[]{:S(2)}) collective-permute-start(bf16[144,256]{1,0:T(8,128)(2,1)S(1)} %get-tuple-element.29), channel_id=1, source_target_pairs={{0,8},{4,12},{8,0},{12,4},{1,9},{5,13},{9,1},{13,5},{2,10},{6,14},... | collective-permute-start | bytes 221192 | tf_op jit(solution)/shard_map/ppermute | solution.py:217
  32.5 5.2 %collective-permute-start.16 = (bf16[128,256]{1,0:T(8,128)(2,1)S(1)}, bf16[128,256]{1,0:T(8,128)(2,1)S(1)}, u32[]{:S(2)}, u32[]{:S(2)}) collective-permute-start(bf16[128,256]{1,0:T(8,128)(2,1)S(1)} %pair_sums.1), channel_id=1, source_target_pairs={{0,8},{4,12},{8,0},{12,4},{1,9},{5,13},{9,1},{13,5},{2,10},{6,14},... | collective-permute-start | bytes 196616 | tf_op jit(solution)/shard_map/ppermute | solution.py:217
  33.4 4.3 %collective-permute-start.21 = (f32[8,128]{1,0:T(8,128)S(1)}, f32[8,128]{1,0:T(8,128)S(1)}, u32[]{:S(2)}, u32[]{:S(2)}) collective-permute-start(f32[8,128]{1,0:T(8,128)S(1)} %all_dots.1.refs_2_), channel_id=1, source_target_pairs={{0,3},{1,2},{2,1},{3,0},{4,7},{5,6},{6,5},{7,4},{8,11},{9,10},{10,... | collective-permute-start | bytes 12296 | tf_op jit(solution)/shard_map/ppermute | solution.py:217
  33.5 4.2 %collective-permute-start.20 = (f32[8,128]{1,0:T(8,128)S(1)}, f32[8,128]{1,0:T(8,128)S(1)}, u32[]{:S(2)}, u32[]{:S(2)}) collective-permute-start(f32[8,128]{1,0:T(8,128)S(1)} %all_dots.1.refs_2_), channel_id=1, source_target_pairs={{0,2},{1,3},{2,0},{3,1},{4,6},{5,7},{6,4},{7,5},{8,10},{9,11},{10,... | collective-permute-start | bytes 12296 | tf_op jit(solution)/shard_map/ppermute | solution.py:217
  35.5 2.2 %collective-permute-start.19 = (f32[8,128]{1,0:T(8,128)S(1)}, f32[8,128]{1,0:T(8,128)S(1)}, u32[]{:S(2)}, u32[]{:S(2)}) collective-permute-start(f32[8,128]{1,0:T(8,128)S(1)} %all_dots.1.refs_2_), channel_id=1, source_target_pairs={{0,1},{1,0},{2,3},{3,2},{4,5},{5,4},{6,7},{7,6},{8,9},{9,8},{10,11... | collective-permute-start | bytes 12296 | tf_op jit(solution)/shard_map/ppermute | solution.py:217

commit v3 on v2

--- a/solution.py
+++ b/solution.py
@@ -239,7 +239,6 @@
     far_sum = swap(pair_sums(parts[5], paired), op, 2)
     terms = terms_of(all_dots(dots, first), ("sec", "help"))
     (sigma_one,) = finish(psi_one.shape, parts[0], first)
-    far_sum, sigma_one = after(far_sum, sigma_one)
     sigma_two, subspace = finish(psi_two.shape, parts[4], [paired, far_sum], terms, scale)
     return sigma_one, sigma_two, subspace
 

time: 38.5 us -> 38.8 us (level)
  starting transfers between devices: 17.3 us -> 18.6 us
  Pallas kernels: 6.26 us -> 5 us
    pallas_call x5, Pallas kernels: 6.26 us -> 5 us  [call(): pl.pallas_call(kernel, out_shape=outs, in_specs=[SCALARS] * n_scalars + [...]
    ppermute x22, starting transfers between devices: 17.3 us -> 18.6 us  [swap(): return lax.ppermute(x, axes, [(i, i ^ hop) for i in range(size)])]
  transfers between devices with their start and end apart: 22 -> 22, of which waited for: 7 -> 9; matrix products, arithmetic and copies ran while one was open for 4% -> 4% of each run, Pallas kernels for 2% -> 2%
where the time goes in v3:
time: 38.8 us; the launch traced here: 38.4 us
  starting transfers between devices  18.6 us (48%)
  waiting for transfers between devices  10.4 us (27%)
  Pallas kernels  5 us (13%)
  local copies, waits for them, and re-layouts  2.9 us (7%)
  between operations  1.42 us (4%)
    ppermute x22, starting transfers between devices, swap(): return lax.ppermute(x, axes, [(i, i ^ hop) for i in range(size)])  18.6 us
    ppermute x22, waiting for transfers between devices, swap(): return lax.ppermute(x, axes, [(i, i ^ hop) for i in range(size)])  10.4 us
    pallas_call x5, Pallas kernels, call(): pl.pallas_call(kernel, out_shape=outs, in_specs=[SCALARS] * n_scalars + [...  5 us
    unnamed x15, local copies, waits for them, and re-layouts  2.9 us
  transfers between devices with their start and end apart: 22, of which 9 were waited for; matrix products, arithmetic and copies ran while one was open for 4% of the time, Pallas kernels for 2%

profile of v3, /device:TPU:0, one launch (start us, length us, event | category | flops | bytes accessed | tf_op | source)
XLA Modules:
  0.0 38.4 jit_solution(4795836427143032762)
XLA Ops:
  0.6 4.1 %collective-permute-start = (bf16[4,32,256]{2,1,0:T(8,128)(2,1)}, bf16[4,32,256]{2,1,0:T(8,128)(2,1)S(1)}, u32[]{:S(2)}, u32[]{:S(2)}) collective-permute-start(bf16[4,32,256]{2,1,0:T(8,128)(2,1)} %refs_0_), channel_id=1, source_target_pairs={{0,8},{4,12},{8,0},{12,4},{1,9},{5,13},{9,1},{13,5},{2,10},{6,14},... | collective-permute-start | bytes 196616 | tf_op jit(solution)/shard_map/ppermute | solution.py:217
  4.7 1.6 %collective-permute-start.2 = (bf16[4,32,256]{2,1,0:T(8,128)(2,1)}, bf16[4,32,256]{2,1,0:T(8,128)(2,1)S(1)}, u32[]{:S(2)}, u32[]{:S(2)}) collective-permute-start(bf16[4,32,256]{2,1,0:T(8,128)(2,1)} %refs_0_), channel_id=1, source_target_pairs={{0,4},{4,0},{8,12},{12,8},{1,5},{5,1},{9,13},{13,9},{2,6},{6,2},{1... | collective-permute-start | bytes 196616 | tf_op jit(solution)/shard_map/ppermute | solution.py:217
  6.3 0.3 collective-permute-start.8
  6.6 0.2 collective-permute-start.7
  7.5 0.6 %copy-done.3 = s32[1,1,64]{2,1,0:T(1,128)S(1)} copy-done((s32[1,1,64]{2,1,0:T(1,128)S(1)}, s32[1,1,64]{2,1,0:T(1,128)}, u32[]{:S(2)}) %copy-start.3) | copy-done | bytes 280
  8.2 1.6 %copy.14 = bf16[8,256,256]{1,2,0:T(8,128)(2,1)S(1)} copy(bf16[8,256,256]{2,1,0:T(8,128)(2,1)} %param.12) | data formatting | bytes 2097152 | tf_op args[3]
  9.8 0.1 collective-permute-start.5
  9.8 1.9 %collective-permute-start.1 = (bf16[4,32,256]{2,1,0:T(8,128)(2,1)S(1)}, bf16[4,32,256]{2,1,0:T(8,128)(2,1)S(1)}, u32[]{:S(2)}, u32[]{:S(2)}) collective-permute-start(bf16[4,32,256]{2,1,0:T(8,128)(2,1)S(1)} %collective-permute-done.refs_2_), channel_id=1, source_target_pairs={{0,4},{4,0},{8,12},{12,8},{1,5},{5,1},{9,13},{13,9},{2,6},{6,2},{1... | collective-permute-start | bytes 196616 | tf_op jit(solution)/shard_map/ppermute | solution.py:217
  11.7 0.6 %collective-permute-done.8.refs_10_ = bf16[4,32,256]{2,1,0:T(8,128)(2,1)S(1)} collective-permute-done((bf16[4,32,256]{2,1,0:T(8,128)(2,1)}, bf16[4,32,256]{2,1,0:T(8,128)(2,1)S(1)}, u32[]{:S(2)}, u32[]{:S(2)}) %collective-permute-start.8) | collective-permute-done | bytes 65568 | tf_op jit(solution)/shard_map/ppermute | solution.py:217
  12.3 0.3 collective-permute-start.9
  12.5 0.3 collective-permute-start.4
  12.9 1.5 %collective-permute-done.1.refs_3_ = bf16[4,32,256]{2,1,0:T(8,128)(2,1)S(1)} collective-permute-done((bf16[4,32,256]{2,1,0:T(8,128)(2,1)S(1)}, bf16[4,32,256]{2,1,0:T(8,128)(2,1)S(1)}, u32[]{:S(2)}, u32[]{:S(2)}) %collective-permute-start.1) | collective-permute-done | bytes 65568 | tf_op jit(solution)/shard_map/ppermute | solution.py:217
  14.4 0.5 %collective-permute-start.3 = (bf16[4,32,256]{2,1,0:T(8,128)(2,1)S(1)}, bf16[4,32,256]{2,1,0:T(8,128)(2,1)S(1)}, u32[]{:S(2)}, u32[]{:S(2)}) collective-permute-start(bf16[4,32,256]{2,1,0:T(8,128)(2,1)S(1)} %copy-done), channel_id=1, source_target_pairs={{0,1},{1,0},{2,3},{3,2},{4,5},{5,4},{6,7},{7,6},{8,9},{9,8},{10,11... | collective-permute-start | bytes 196616 | tf_op jit(solution)/shard_map/ppermute | solution.py:217
  14.9 0.1 collective-permute-start.6
  15.0 0.4 %collective-permute-start.10 = (bf16[4,32,256]{2,1,0:T(8,128)(2,1)S(1)}, bf16[4,32,256]{2,1,0:T(8,128)(2,1)S(1)}, u32[]{:S(2)}, u32[]{:S(2)}) collective-permute-start(bf16[4,32,256]{2,1,0:T(8,128)(2,1)S(1)} %copy-done.1), channel_id=1, source_target_pairs={{0,1},{1,0},{2,3},{3,2},{4,5},{5,4},{6,7},{7,6},{8,9},{9,8},{10,11... | collective-permute-start | bytes 196616 | tf_op jit(solution)/shard_map/ppermute | solution.py:217
  15.5 1.3 %collective-permute-done.9.refs_11_ = bf16[4,32,256]{2,1,0:T(8,128)(2,1)S(1)} collective-permute-done((bf16[4,32,256]{2,1,0:T(8,128)(2,1)S(1)}, bf16[4,32,256]{2,1,0:T(8,128)(2,1)S(1)}, u32[]{:S(2)}, u32[]{:S(2)}) %collective-permute-start.9) | collective-permute-done | bytes 65568 | tf_op jit(solution)/shard_map/ppermute | solution.py:217
  16.8 0.7 %copy-done.5 = s32[1,1,64]{2,1,0:T(1,128)S(1)} copy-done((s32[1,1,64]{2,1,0:T(1,128)S(1)}, s32[1,1,64]{2,1,0:T(1,128)}, u32[]{:S(2)}) %copy-start.5) | copy-done | bytes 280
  17.5 0.5 %collective-permute-done.13.refs_15_ = bf16[4,32,256]{2,1,0:T(8,128)(2,1)S(1)} collective-permute-done((bf16[4,32,256]{2,1,0:T(8,128)(2,1)S(1)}, bf16[4,32,256]{2,1,0:T(8,128)(2,1)S(1)}, u32[]{:S(2)}, u32[]{:S(2)}) %collective-permute-start.13) | collective-permute-done | bytes 65568 | tf_op jit(solution)/shard_map/ppermute | solution.py:217
  18.1 3.6 %products.1 = (f32[128,256]{1,0:T(8,128)S(1)}, bf16[144,256]{1,0:T(8,128)(2,1)S(1)}, bf16[144,256]{1,0:T(8,128)(2,1)S(1)}, bf16[144,256]{1,0:T(8,128)(2,1)S(1)},...) custom-call(s32[4,64]{1,0:T(4,128)S(1)} %pad_add_fusion.table, ...), custom_call_target="tpu_custom_call" | custom-call | tf_op jit(solution)/shard_map/products/pallas_call | solution.py:19
  21.6 2.2 %collective-permute-start.16 = (bf16[256,256]{1,0:T(8,128)(2,1)S(1)}, bf16[256,256]{1,0:T(8,128)(2,1)S(1)}, u32[]{:S(2)}, u32[]{:S(2)}) collective-permute-start(bf16[256,256]{1,0:T(8,128)(2,1)S(1)} %get-tuple-element.24), channel_id=1, source_target_pairs={{0,4},{4,0},{8,12},{12,8},{1,5},{5,1},{9,13},{13,9},{2,6},{6,2},{1... | collective-permute-start | bytes 393224 | tf_op jit(solution)/shard_map/ppermute | solution.py:217
  23.8 2.6 %collective-permute-start.17 = (bf16[144,256]{1,0:T(8,128)(2,1)S(1)}, bf16[144,256]{1,0:T(8,128)(2,1)S(1)}, u32[]{:S(2)}, u32[]{:S(2)}) collective-permute-start(bf16[144,256]{1,0:T(8,128)(2,1)S(1)} %get-tuple-element.25), channel_id=1, source_target_pairs={{0,12},{4,8},{8,4},{12,0},{1,13},{5,9},{9,5},{13,1},{2,14},{6,10},... | collective-permute-start | bytes 221192 | tf_op jit(solution)/shard_map/ppermute | solution.py:217
  26.5 1.8 %collective-permute-start.15 = (bf16[144,256]{1,0:T(8,128)(2,1)S(1)}, bf16[144,256]{1,0:T(8,128)(2,1)S(1)}, u32[]{:S(2)}, u32[]{:S(2)}) collective-permute-start(bf16[144,256]{1,0:T(8,128)(2,1)S(1)} %get-tuple-element.23), channel_id=1, source_target_pairs={{0,8},{4,12},{8,0},{12,4},{1,9},{5,13},{9,1},{13,5},{2,10},{6,14},... | collective-permute-start | bytes 221192 | tf_op jit(solution)/shard_map/ppermute | solution.py:217
  28.2 4.2 %collective-permute-done.17.refs_2_ = bf16[144,256]{1,0:T(8,128)(2,1)S(1)} collective-permute-done((bf16[144,256]{1,0:T(8,128)(2,1)S(1)}, bf16[144,256]{1,0:T(8,128)(2,1)S(1)}, u32[]{:S(2)}, u32[]{:S(2)}) %collective-permute-start.17) | collective-permute-done | bytes 73760 | tf_op jit(solution)/shard_map/ppermute | solution.py:217
  32.5 0.1 collective-permute-start.18
  32.5 0.9 %collective-permute-done.14.refs_0_ = bf16[144,256]{1,0:T(8,128)(2,1)S(1)} collective-permute-done((bf16[144,256]{1,0:T(8,128)(2,1)S(1)}, bf16[144,256]{1,0:T(8,128)(2,1)S(1)}, u32[]{:S(2)}, u32[]{:S(2)}) %collective-permute-start.14) | collective-permute-done | bytes 73760 | tf_op jit(solution)/shard_map/ppermute | solution.py:217
  33.4 0.1 collective-permute-start.21
  33.5 2.0 %collective-permute-start.20 = (f32[8,128]{1,0:T(8,128)S(1)}, f32[8,128]{1,0:T(8,128)S(1)}, u32[]{:S(2)}, u32[]{:S(2)}) collective-permute-start(f32[8,128]{1,0:T(8,128)S(1)} %all_dots.1.refs_2_), channel_id=1, source_target_pairs={{0,2},{1,3},{2,0},{3,1},{4,6},{5,7},{6,4},{7,5},{8,10},{9,11},{10,... | collective-permute-start | bytes 12296 | tf_op jit(solution)/shard_map/ppermute | solution.py:217
  35.6 0.7 %finish.2 = f32[4,32,256]{2,1,0:T(8,128)} custom-call(f32[128,256]{1,0:T(8,128)S(1)} %get-tuple-element.21.mine, bf16[144,256]{1,0:T(8,128)(2,1)S(1)} %collective-permute-done.14.refs_0_, bf16[144,256]{1,0:T(8,128)(2,1)S(1)} %collective-permute-done.15.refs_1_, bf16[144,256]{1,0:T(8,128)(2,1)S(1)} %collective-permute-done.17.refs_2_), custom_call_target="tpu_custom_call" | custom-call | tf_op jit(solution)/shard_map/finish/pallas_call | solution.py:19
  36.3 0.3 collective-permute-done.21.refs_5_
  36.5 0.7 %collective-permute-done.20.refs_4_ = f32[8,128]{1,0:T(8,128)S(1)} collective-permute-done((f32[8,128]{1,0:T(8,128)S(1)}, f32[8,128]{1,0:T(8,128)S(1)}, u32[]{:S(2)}, u32[]{:S(2)}) %collective-permute-start.20) | collective-permute-done | bytes 4128 | tf_op jit(solution)/shard_map/ppermute | solution.py:217
  37.2 0.5 %collective-permute-done.18.refs_1_ = bf16[128,256]{1,0:T(8,128)(2,1)S(1)} collective-permute-done((bf16[128,256]{1,0:T(8,128)(2,1)S(1)}, bf16[128,256]{1,0:T(8,128)(2,1)S(1)}, u32[]{:S(2)}, u32[]{:S(2)}) %collective-permute-start.18) | collective-permute-done | bytes 65568 | tf_op jit(solution)/shard_map/ppermute | solution.py:217
  37.7 0.7 %finish.3 = (f32[4,32,256]{2,1,0:T(8,128)}, f32[2,2]{1,0:T(2,128)}) custom-call(f32[128,256]{1,0:T(8,128)S(1)} %get-tuple-element.27.mine, bf16[256,256]{1,0:T(8,128)(2,1)S(1)} %collective-permute-done.16.received.refs_0_, bf16[128,256]{1,0:T(8,128)(2,1)S(1)} %collective-permute-done.18.refs_1_, f32[8,128]{1,0:T(8,128)S(1)} %all_dots.1.refs_2_, ...), custom_call_target="tpu_custom_call" | custom-call | tf_op jit(solution)/shard_map/finish/pallas_call | solution.py:19
  (35 shorter events, 0.2 us)
Async XLA Ops:
  0.6 9.1 %collective-permute-start = (bf16[4,32,256]{2,1,0:T(8,128)(2,1)}, bf16[4,32,256]{2,1,0:T(8,128)(2,1)S(1)}, u32[]{:S(2)}, u32[]{:S(2)}) collective-permute-start(bf16[4,32,256]{2,1,0:T(8,128)(2,1)} %refs_0_), channel_id=1, source_target_pairs={{0,8},{4,12},{8,0},{12,4},{1,9},{5,13},{9,1},{13,5},{2,10},{6,14},... | collective-permute-start | bytes 196616 | tf_op jit(solution)/shard_map/ppermute | solution.py:217
  4.7 7.6 %collective-permute-start.2 = (bf16[4,32,256]{2,1,0:T(8,128)(2,1)}, bf16[4,32,256]{2,1,0:T(8,128)(2,1)S(1)}, u32[]{:S(2)}, u32[]{:S(2)}) collective-permute-start(bf16[4,32,256]{2,1,0:T(8,128)(2,1)} %refs_0_), channel_id=1, source_target_pairs={{0,4},{4,0},{8,12},{12,8},{1,5},{5,1},{9,13},{13,9},{2,6},{6,2},{1... | collective-permute-start | bytes 196616 | tf_op jit(solution)/shard_map/ppermute | solution.py:217
  6.3 6.0 %collective-permute-start.8 = (bf16[4,32,256]{2,1,0:T(8,128)(2,1)}, bf16[4,32,256]{2,1,0:T(8,128)(2,1)S(1)}, u32[]{:S(2)}, u32[]{:S(2)}) collective-permute-start(bf16[4,32,256]{2,1,0:T(8,128)(2,1)} %refs_8_), channel_id=1, source_target_pairs={{0,8},{4,12},{8,0},{12,4},{1,9},{5,13},{9,1},{13,5},{2,10},{6,14},... | collective-permute-start | bytes 196616 | tf_op jit(solution)/shard_map/ppermute | solution.py:217
  6.6 5.9 %collective-permute-start.7 = (bf16[4,32,256]{2,1,0:T(8,128)(2,1)}, bf16[4,32,256]{2,1,0:T(8,128)(2,1)S(1)}, u32[]{:S(2)}, u32[]{:S(2)}) collective-permute-start(bf16[4,32,256]{2,1,0:T(8,128)(2,1)} %refs_8_), channel_id=1, source_target_pairs={{0,4},{4,0},{8,12},{12,8},{1,5},{5,1},{9,13},{13,9},{2,6},{6,2},{1... | collective-permute-start | bytes 196616 | tf_op jit(solution)/shard_map/ppermute | solution.py:217
  7.5 0.7 %copy-start.3 = (s32[1,1,64]{2,1,0:T(1,128)S(1)}, s32[1,1,64]{2,1,0:T(1,128)}, u32[]{:S(2)}) copy-start(s32[1,1,64]{2,1,0:T(1,128)} %param.15) | copy-start | bytes 772
  7.5 0.7 %copy-start.4 = (s32[1,1,64]{2,1,0:T(1,128)S(1)}, s32[1,1,64]{2,1,0:T(1,128)}, u32[]{:S(2)}) copy-start(s32[1,1,64]{2,1,0:T(1,128)} %param.13) | copy-start | bytes 772
  8.2 4.7 %copy-start.2 = (bf16[8,256,256]{2,1,0:T(8,128)(2,1)S(1)}, bf16[8,256,256]{2,1,0:T(8,128)(2,1)}, u32[]{:S(2)}) copy-start(bf16[8,256,256]{2,1,0:T(8,128)(2,1)} %param.11) | copy-start | bytes 3145732
  9.8 4.7 %collective-permute-start.5 = (bf16[4,32,256]{2,1,0:T(8,128)(2,1)S(1)}, bf16[4,32,256]{2,1,0:T(8,128)(2,1)S(1)}, u32[]{:S(2)}, u32[]{:S(2)}) collective-permute-start(bf16[4,32,256]{2,1,0:T(8,128)(2,1)S(1)} %collective-permute-done.refs_2_), channel_id=1, source_target_pairs={{0,1},{1,0},{2,3},{3,2},{4,5},{5,4},{6,7},{7,6},{8,9},{9,8},{10,11... | collective-permute-start | bytes 196616 | tf_op jit(solution)/shard_map/ppermute | solution.py:217
  9.8 4.6 %collective-permute-start.1 = (bf16[4,32,256]{2,1,0:T(8,128)(2,1)S(1)}, bf16[4,32,256]{2,1,0:T(8,128)(2,1)S(1)}, u32[]{:S(2)}, u32[]{:S(2)}) collective-permute-start(bf16[4,32,256]{2,1,0:T(8,128)(2,1)S(1)} %collective-permute-done.refs_2_), channel_id=1, source_target_pairs={{0,4},{4,0},{8,12},{12,8},{1,5},{5,1},{9,13},{13,9},{2,6},{6,2},{1... | collective-permute-start | bytes 196616 | tf_op jit(solution)/shard_map/ppermute | solution.py:217
  12.3 2.7 %collective-permute-start.12 = (bf16[4,32,256]{2,1,0:T(8,128)(2,1)S(1)}, bf16[4,32,256]{2,1,0:T(8,128)(2,1)S(1)}, u32[]{:S(2)}, u32[]{:S(2)}) collective-permute-start(bf16[4,32,256]{2,1,0:T(8,128)(2,1)S(1)} %collective-permute-done.8.refs_10_), channel_id=1, source_target_pairs={{0,1},{1,0},{2,3},{3,2},{4,5},{5,4},{6,7},{7,6},{8,9},{9,8},{10,11... | collective-permute-start | bytes 196616 | tf_op jit(solution)/shard_map/ppermute | solution.py:217
  12.3 4.5 %collective-permute-start.9 = (bf16[4,32,256]{2,1,0:T(8,128)(2,1)S(1)}, bf16[4,32,256]{2,1,0:T(8,128)(2,1)S(1)}, u32[]{:S(2)}, u32[]{:S(2)}) collective-permute-start(bf16[4,32,256]{2,1,0:T(8,128)(2,1)S(1)} %collective-permute-done.8.refs_10_), channel_id=1, source_target_pairs={{0,4},{4,0},{8,12},{12,8},{1,5},{5,1},{9,13},{13,9},{2,6},{6,2},{1... | collective-permute-start | bytes 196616 | tf_op jit(solution)/shard_map/ppermute | solution.py:217
  12.5 2.4 %collective-permute-start.4 = (bf16[4,32,256]{2,1,0:T(8,128)(2,1)S(1)}, bf16[4,32,256]{2,1,0:T(8,128)(2,1)S(1)}, u32[]{:S(2)}, u32[]{:S(2)}) collective-permute-start(bf16[4,32,256]{2,1,0:T(8,128)(2,1)S(1)} %collective-permute-done.2.refs_1_), channel_id=1, source_target_pairs={{0,1},{1,0},{2,3},{3,2},{4,5},{5,4},{6,7},{7,6},{8,9},{9,8},{10,11... | collective-permute-start | bytes 196616 | tf_op jit(solution)/shard_map/ppermute | solution.py:217
  12.9 1.6 %copy-start = (bf16[4,32,256]{2,1,0:T(8,128)(2,1)S(1)}, bf16[4,32,256]{2,1,0:T(8,128)(2,1)}, u32[]{:S(2)}) copy-start(bf16[4,32,256]{2,1,0:T(8,128)(2,1)} %refs_0_) | copy-start | bytes 196612
  12.9 2.1 %copy-start.1 = (bf16[4,32,256]{2,1,0:T(8,128)(2,1)S(1)}, bf16[4,32,256]{2,1,0:T(8,128)(2,1)}, u32[]{:S(2)}) copy-start(bf16[4,32,256]{2,1,0:T(8,128)(2,1)} %refs_8_) | copy-start | bytes 196612
  14.4 3.1 %collective-permute-start.11 = (bf16[4,32,256]{2,1,0:T(8,128)(2,1)S(1)}, bf16[4,32,256]{2,1,0:T(8,128)(2,1)S(1)}, u32[]{:S(2)}, u32[]{:S(2)}) collective-permute-start(bf16[4,32,256]{2,1,0:T(8,128)(2,1)S(1)} %collective-permute-done.7.refs_9_), channel_id=1, source_target_pairs={{0,1},{1,0},{2,3},{3,2},{4,5},{5,4},{6,7},{7,6},{8,9},{9,8},{10,11... | collective-permute-start | bytes 196616 | tf_op jit(solution)/shard_map/ppermute | solution.py:217
  14.4 3.1 %collective-permute-start.3 = (bf16[4,32,256]{2,1,0:T(8,128)(2,1)S(1)}, bf16[4,32,256]{2,1,0:T(8,128)(2,1)S(1)}, u32[]{:S(2)}, u32[]{:S(2)}) collective-permute-start(bf16[4,32,256]{2,1,0:T(8,128)(2,1)S(1)} %copy-done), channel_id=1, source_target_pairs={{0,1},{1,0},{2,3},{3,2},{4,5},{5,4},{6,7},{7,6},{8,9},{9,8},{10,11... | collective-permute-start | bytes 196616 | tf_op jit(solution)/shard_map/ppermute | solution.py:217
  14.9 2.6 %collective-permute-start.6 = (bf16[4,32,256]{2,1,0:T(8,128)(2,1)S(1)}, bf16[4,32,256]{2,1,0:T(8,128)(2,1)S(1)}, u32[]{:S(2)}, u32[]{:S(2)}) collective-permute-start(bf16[4,32,256]{2,1,0:T(8,128)(2,1)S(1)} %collective-permute-done.1.refs_3_), channel_id=1, source_target_pairs={{0,1},{1,0},{2,3},{3,2},{4,5},{5,4},{6,7},{7,6},{8,9},{9,8},{10,11... | collective-permute-start | bytes 196616 | tf_op jit(solution)/shard_map/ppermute | solution.py:217
  15.0 2.5 %collective-permute-start.10 = (bf16[4,32,256]{2,1,0:T(8,128)(2,1)S(1)}, bf16[4,32,256]{2,1,0:T(8,128)(2,1)S(1)}, u32[]{:S(2)}, u32[]{:S(2)}) collective-permute-start(bf16[4,32,256]{2,1,0:T(8,128)(2,1)S(1)} %copy-done.1), channel_id=1, source_target_pairs={{0,1},{1,0},{2,3},{3,2},{4,5},{5,4},{6,7},{7,6},{8,9},{9,8},{10,11... | collective-permute-start | bytes 196616 | tf_op jit(solution)/shard_map/ppermute | solution.py:217
  16.8 1.3 %collective-permute-start.13 = (bf16[4,32,256]{2,1,0:T(8,128)(2,1)S(1)}, bf16[4,32,256]{2,1,0:T(8,128)(2,1)S(1)}, u32[]{:S(2)}, u32[]{:S(2)}) collective-permute-start(bf16[4,32,256]{2,1,0:T(8,128)(2,1)S(1)} %collective-permute-done.9.refs_11_), channel_id=1, source_target_pairs={{0,1},{1,0},{2,3},{3,2},{4,5},{5,4},{6,7},{7,6},{8,9},{9,8},{10,11... | collective-permute-start | bytes 196616 | tf_op jit(solution)/shard_map/ppermute | solution.py:217
  16.8 0.7 %copy-start.5 = (s32[1,1,64]{2,1,0:T(1,128)S(1)}, s32[1,1,64]{2,1,0:T(1,128)}, u32[]{:S(2)}) copy-start(s32[1,1,64]{2,1,0:T(1,128)} %param.14) | copy-start | bytes 772
  16.8 0.7 %copy-start.6 = (s32[1,1,64]{2,1,0:T(1,128)S(1)}, s32[1,1,64]{2,1,0:T(1,128)}, u32[]{:S(2)}) copy-start(s32[1,1,64]{2,1,0:T(1,128)} %param.16) | copy-start | bytes 772
  21.6 10.8 %collective-permute-start.16 = (bf16[256,256]{1,0:T(8,128)(2,1)S(1)}, bf16[256,256]{1,0:T(8,128)(2,1)S(1)}, u32[]{:S(2)}, u32[]{:S(2)}) collective-permute-start(bf16[256,256]{1,0:T(8,128)(2,1)S(1)} %get-tuple-element.24), channel_id=1, source_target_pairs={{0,4},{4,0},{8,12},{12,8},{1,5},{5,1},{9,13},{13,9},{2,6},{6,2},{1... | collective-permute-start | bytes 393224 | tf_op jit(solution)/shard_map/ppermute | solution.py:217
  23.8 8.6 %collective-permute-start.17 = (bf16[144,256]{1,0:T(8,128)(2,1)S(1)}, bf16[144,256]{1,0:T(8,128)(2,1)S(1)}, u32[]{:S(2)}, u32[]{:S(2)}) collective-permute-start(bf16[144,256]{1,0:T(8,128)(2,1)S(1)} %get-tuple-element.25), channel_id=1, source_target_pairs={{0,12},{4,8},{8,4},{12,0},{1,13},{5,9},{9,5},{13,1},{2,14},{6,10},... | collective-permute-start | bytes 221192 | tf_op jit(solution)/shard_map/ppermute | solution.py:217
  26.5 6.9 %collective-permute-start.14 = (bf16[144,256]{1,0:T(8,128)(2,1)S(1)}, bf16[144,256]{1,0:T(8,128)(2,1)S(1)}, u32[]{:S(2)}, u32[]{:S(2)}) collective-permute-start(bf16[144,256]{1,0:T(8,128)(2,1)S(1)} %get-tuple-element.22), channel_id=1, source_target_pairs={{0,4},{4,0},{8,12},{12,8},{1,5},{5,1},{9,13},{13,9},{2,6},{6,2},{1... | collective-permute-start | bytes 221192 | tf_op jit(solution)/shard_map/ppermute | solution.py:217
  26.5 6.9 %collective-permute-start.15 = (bf16[144,256]{1,0:T(8,128)(2,1)S(1)}, bf16[144,256]{1,0:T(8,128)(2,1)S(1)}, u32[]{:S(2)}, u32[]{:S(2)}) collective-permute-start(bf16[144,256]{1,0:T(8,128)(2,1)S(1)} %get-tuple-element.23), channel_id=1, source_target_pairs={{0,8},{4,12},{8,0},{12,4},{1,9},{5,13},{9,1},{13,5},{2,10},{6,14},... | collective-permute-start | bytes 221192 | tf_op jit(solution)/shard_map/ppermute | solution.py:217
  32.5 5.2 %collective-permute-start.18 = (bf16[128,256]{1,0:T(8,128)(2,1)S(1)}, bf16[128,256]{1,0:T(8,128)(2,1)S(1)}, u32[]{:S(2)}, u32[]{:S(2)}) collective-permute-start(bf16[128,256]{1,0:T(8,128)(2,1)S(1)} %pair_sums.1), channel_id=1, source_target_pairs={{0,8},{4,12},{8,0},{12,4},{1,9},{5,13},{9,1},{13,5},{2,10},{6,14},... | collective-permute-start | bytes 196616 | tf_op jit(solution)/shard_map/ppermute | solution.py:217
  33.4 3.1 %collective-permute-start.21 = (f32[8,128]{1,0:T(8,128)S(1)}, f32[8,128]{1,0:T(8,128)S(1)}, u32[]{:S(2)}, u32[]{:S(2)}) collective-permute-start(f32[8,128]{1,0:T(8,128)S(1)} %all_dots.1.refs_2_), channel_id=1, source_target_pairs={{0,3},{1,2},{2,1},{3,0},{4,7},{5,6},{6,5},{7,4},{8,11},{9,10},{10,... | collective-permute-start | bytes 12296 | tf_op jit(solution)/shard_map/ppermute | solution.py:217
  33.5 3.7 %collective-permute-start.20 = (f32[8,128]{1,0:T(8,128)S(1)}, f32[8,128]{1,0:T(8,128)S(1)}, u32[]{:S(2)}, u32[]{:S(2)}) collective-permute-start(f32[8,128]{1,0:T(8,128)S(1)} %all_dots.1.refs_2_), channel_id=1, source_target_pairs={{0,2},{1,3},{2,0},{3,1},{4,6},{5,7},{6,4},{7,5},{8,10},{9,11},{10,... | collective-permute-start | bytes 12296 | tf_op jit(solution)/shard_map/ppermute | solution.py:217
  35.5 1.7 %collective-permute-start.19 = (f32[8,128]{1,0:T(8,128)S(1)}, f32[8,128]{1,0:T(8,128)S(1)}, u32[]{:S(2)}, u32[]{:S(2)}) collective-permute-start(f32[8,128]{1,0:T(8,128)S(1)} %all_dots.1.refs_2_), channel_id=1, source_target_pairs={{0,1},{1,0},{2,3},{3,2},{4,5},{5,4},{6,7},{7,6},{8,9},{9,8},{10,11... | collective-permute-start | bytes 12296 | tf_op jit(solution)/shard_map/ppermute | solution.py:217
